TPU v7x, 256 devices: a whole 4x4x8 slice. The times are simulated.
256 devices in a mesh: set: 8 (over x, y_lo), dp: 32 (over z, y_hi, core).
Axes of the slice: x: 4, y: 4 (y_hi: 2, y_lo: 2; y = y_hi * 2 + y_lo), z: 8, core: 2. Of those that a mesh axis runs over, the one named last changes fastest.
Arguments:
- embeddings: bfloat16 [16, 4096, 1024], P('set', 'dp'), may hold values from -0.75 to 0.75
- cotangent: bfloat16 [4096, 8192], P('dp', 'set'), may hold values from -0.625 to 0.625
- first_weight: bfloat16 [1920, 8192], P('set'), may hold values from -0.5 to 0.5
- feature_rows: int32 [4096, 16], P('dp'), may hold values from 0 to 16383, as said below
Outputs:
- weight_grad: bfloat16 [1920, 8192], P('set', 'dp')
- table_grad: float32 [16384, 1024], P('dp', 'set')
Inputs may be any that keep to these rules, and one draw needn't show every extreme that they name: `feature_rows`: row r is kept by owner r // 512. Among the 2048 ids of each aligned block of 128 samples, one owner, the same for all blocks, holds exactly 128, and every other owner holds as many as any other, up to one.
All inputs are finite; a program needn't handle non-finite values.
Results may differ from a plain program's by a relative error of at most 0.0075.
Values may be sent and summed in bfloat16 or wider, within the bound.
A program may use at most 64 MiB of HBM per device.

v0:
```python
import math

import jax
import jax.numpy as jnp
import numpy as np
from jax import lax
from jax.sharding import PartitionSpec as P

K = 64
F = 16
ROWS_DEV = 512


def pair_table(width):
    first_feature, second_feature = np.triu_indices(width, 1)
    flat_pairs = first_feature * width + second_feature
    table_np = (np.arange(width * width)[:, None] == flat_pairs[None, :]).astype(np.float32)
    return jnp.asarray(table_np)


def build_slots(item_values, flat_rows, dp_count, capacity):
    item_count = flat_rows.shape[0]
    row_width = item_values.shape[1]
    block_size = min(256, item_count)
    blocks = item_count // block_size
    owner_of = flat_rows // ROWS_DEV
    local_row = flat_rows - owner_of * ROWS_DEV
    owner_ids = jnp.arange(dp_count, dtype=jnp.int32)
    owner_hot = (
        owner_of.reshape(blocks, block_size)[:, :, None] == owner_ids[None, None, :]
    ).astype(jnp.float32)
    positions = jnp.arange(block_size, dtype=jnp.int32)
    earlier_mask = (positions[None, :] < positions[:, None]).astype(jnp.float32)
    earlier_count = jnp.einsum(
        "ij,bjo->bio", earlier_mask, owner_hot, precision=lax.Precision.HIGHEST
    )
    rank_within = jnp.sum(earlier_count * owner_hot, axis=2)
    counts = jnp.sum(owner_hot, axis=1)
    owner_start = jnp.cumsum(counts, axis=1) - counts
    block_place = (jnp.sum(owner_start[:, None, :] * owner_hot, axis=2) + rank_within).astype(
        jnp.int32
    )
    placement = block_place[:, None, :] == positions[None, :, None]
    values_blocks = item_values.reshape(blocks, block_size, row_width)
    compact_values = (
        jnp.einsum(
            "bpi,bik->bpk",
            placement.astype(jnp.bfloat16),
            values_blocks,
            preferred_element_type=jnp.float32,
        )
        .astype(jnp.bfloat16)
        .reshape(item_count, row_width)
    )
    compact_rows = jnp.sum(
        placement.astype(jnp.int32) * local_row.reshape(blocks, 1, block_size), axis=2
    ).reshape(-1)
    counts_int = counts.astype(jnp.int32)
    before = jnp.cumsum(counts_int, axis=0) - counts_int
    block_ends = before + counts_int
    rank_slots = jnp.arange(capacity, dtype=jnp.int32)
    chosen = jnp.sum(
        (block_ends.T[:, None, :] <= rank_slots[None, :, None]).astype(jnp.int32), axis=2
    )
    chosen = jnp.minimum(chosen, blocks - 1)
    is_live = rank_slots[None, :] < block_ends[blocks - 1][:, None]
    start_of = jnp.take_along_axis(before.T, chosen, axis=1)
    offset_of = jnp.take_along_axis(owner_start.astype(jnp.int32).T, chosen, axis=1)
    source = chosen * block_size + offset_of + rank_slots[None, :] - start_of
    source = jnp.where(is_live, source, 0)
    send_values = jnp.where(
        is_live[:, :, None], jnp.take(compact_values, source, axis=0), jnp.zeros((), jnp.bfloat16)
    )
    send_rows = jnp.where(is_live, jnp.take(compact_rows, source, axis=0), 0)
    return (send_values, send_rows)


def accumulate_rows(slot_values, slot_rows, dp_count):
    capacity = slot_rows.shape[1]
    row_width = slot_values.shape[2]
    group_size = math.gcd(dp_count, 8)
    turns = dp_count // group_size
    values_grouped = slot_values.reshape(turns, group_size * capacity, row_width)
    rows_grouped = slot_rows.reshape(turns, group_size * capacity)
    local_ids = jnp.arange(ROWS_DEV, dtype=jnp.int32)

    def add_group(running, operands):
        part_values, part_rows = operands
        row_hot = (part_rows[:, None] == local_ids[None, :]).astype(jnp.bfloat16)
        return (
            running
            + lax.dot_general(
                row_hot, part_values, (((0,), (0,)), ((), ())), preferred_element_type=jnp.float32
            ),
            None,
        )

    total, _ = lax.scan(
        add_group, jnp.zeros((ROWS_DEV, row_width), jnp.float32), (values_grouped, rows_grouped)
    )
    return total


def on_device(embeddings, cotangent, first_weight, feature_rows):
    sets_here = embeddings.shape[0]
    group_rows = embeddings.shape[1]
    dp_count = lax.axis_size("dp")
    selector = pair_table(F)
    pair_count = selector.shape[1]
    spread_table = selector.T.astype(jnp.bfloat16)
    full_cotangent = lax.all_gather(cotangent, "set", axis=1, tiled=True)
    pair_list = []
    grad_list = []
    for set_index in range(sets_here):
        embedded = embeddings[set_index].reshape(group_rows, F, K)
        gram_flat = jnp.einsum(
            "bfk,bgk->bfg", embedded, embedded, preferred_element_type=jnp.float32
        ).reshape(group_rows, F * F)
        pairs = jnp.dot(gram_flat, selector, precision=lax.Precision.HIGHEST).astype(jnp.bfloat16)
        weight_block = first_weight[set_index * pair_count : (set_index + 1) * pair_count]
        pair_grad = lax.dot_general(
            full_cotangent,
            weight_block,
            (((1,), (1,)), ((), ())),
            preferred_element_type=jnp.float32,
        ).astype(jnp.bfloat16)
        spread = jnp.dot(pair_grad, spread_table, preferred_element_type=jnp.float32).reshape(
            group_rows, F, F
        )
        symmetric = (spread + jnp.swapaxes(spread, 1, 2)).astype(jnp.bfloat16)
        emb_grad = jnp.einsum(
            "bfg,bgk->bfk", symmetric, embedded, preferred_element_type=jnp.float32
        ).astype(jnp.bfloat16)
        pair_list.append(pairs)
        grad_list.append(emb_grad)
    pairs_all = jnp.concatenate(pair_list, axis=1)
    weight_terms = lax.dot_general(
        pairs_all, full_cotangent, (((0,), (0,)), ((), ())), preferred_element_type=jnp.float32
    )
    weight_grad = lax.psum_scatter(weight_terms, "dp", scatter_dimension=1, tiled=True).astype(
        jnp.bfloat16
    )
    item_values = jnp.stack(grad_list, axis=2).reshape(group_rows * F, sets_here * K)
    flat_rows = feature_rows.reshape(-1)
    item_count = group_rows * F
    capacity = 2 * item_count // dp_count
    send_values, send_rows = build_slots(item_values, flat_rows, dp_count, capacity)
    flat_values = send_values.reshape(dp_count * capacity, sets_here * K)
    flat_slot_rows = send_rows.reshape(dp_count * capacity)
    got_values, got_rows = (
        lax.all_to_all(flat_values, "dp", split_axis=0, concat_axis=0, tiled=True),
        lax.all_to_all(flat_slot_rows, "dp", split_axis=0, concat_axis=0, tiled=True),
    )
    table_grad = accumulate_rows(
        got_values.reshape(dp_count, capacity, sets_here * K),
        got_rows.reshape(dp_count, capacity),
        dp_count,
    )
    return (weight_grad, table_grad)


def solution(mesh):
    return jax.shard_map(
        on_device,
        mesh=mesh,
        in_specs=(P("set", "dp", None), P("dp", "set"), P("set", None), P("dp", None)),
        out_specs=(P("set", "dp"), P("dp", "set")),
        check_vma=False,
    )
```

profile of v0, /device:TPU:1, one launch (start us, length us, event | category | flops | bytes accessed | tf_op | source)
XLA Modules:
  0.0 227.4 jit_solution(17219535680211752412)
XLA Ops:
  7.2 0.7 all-gather.2.cloned.1.call-update
  7.9 1.1 fusion.49
  12.6 53.9 %all-gather.2.cloned.1.call-done = bf16[128,8192]{1,0:T(8,128)(2,1)} async-done(((bf16[128,1024]{1,0:T(8,128)(2,1)}), bf16[128,8192]{1,0:T(8,128)(2,1)}) %all-gather.2.cloned.1.call-update) | async-done | bytes 2097168 | tf_op jit(solution)/shard_map/all_gather | solution.py:111
  66.5 5.8 %fusion.36 = f32[240,8192]{1,0:T(8,128)} fusion(bf16[128,8192]{1,0:T(8,128)(2,1)} %all-gather.2.cloned.1.call-done, bf16[128,120]{0,1:T(8,128)(2,1)S(1)} %convolution_convert_fusion.2, bf16[128,120]{0,1:T(8,128)(2,1)S(1)} %convolution_convert_fusion.3), kind=kOutput, calls=%fused_computation.49 | convolution fusion | flops 503439360 | bytes 10022912 | tf_op jit(solution)/shard_map/dot_general | solution.py:137
  74.7 17.4 %gather_fusion.3 = s32[4096]{0:T(1024)S(1)} fusion(s32[32,8]{0,1:T(8,128)S(1)} %bitcast_subtract_fusion, s32[4096]{0:T(1024)S(1)} %fusion.45), kind=kCustom, calls=%fused_computation.1.clone | custom fusion | bytes 65536 | tf_op jit(solution)/shard_map/jit(take_along_axis)/gather | solution.py:67
  92.1 17.4 %gather_fusion.2 = s32[4096]{0:T(1024)S(1)} fusion(s32[32,8]{0,1:T(8,128)S(1)} %get-tuple-element.60, s32[4096]{0:T(1024)S(1)} %fusion.45), kind=kCustom, calls=%fused_computation.clone | custom fusion | bytes 65536 | tf_op jit(solution)/shard_map/jit(take_along_axis)/gather | solution.py:68
  109.6 23.0 %gather_fusion = s32[4096]{0:T(1024)S(1)} fusion(s32[2048]{0:T(1024)S(1)} %bitcast.102, s32[4096]{0:T(1024)S(1)} %get-tuple-element.58), kind=kCustom, calls=%fused_computation.2 | custom fusion | bytes 49152 | tf_op jit(solution)/shard_map/jit(_take)/gather | solution.py:74
  132.6 0.7 fusion.40
  133.3 10.7 %all-to-all-start = ((s32[32,128,1]{1,2,0:T(1,128)}), s32[32,128,1]{1,2,0:T(1,128)S(1)}, u32[]{:S(2)}, u32[]{:S(2)}) async-start(s32[32,128,1]{1,2,0:T(1,128)} %bitcast.19), calls=%async_computation.1 | async-start | bytes 32768 | tf_op jit(solution)/shard_map/all_to_all | solution.py:152
  144.1 2.5 %fusion.28 = f32[128,256]{0,1:T(8,128)S(1)} fusion(bf16[256,120]{1,0:T(8,128)(2,1)S(1)} %copy-done.4, bf16[128,8192]{1,0:T(8,128)(2,1)S(1)} %copy-done, bf16[240,8192]{1,0:T(8,128)(2,1)} %param.11), kind=kOutput, calls=%fused_computation.33 | convolution fusion | flops 259537920 | bytes 4255744 | tf_op jit(solution)/shard_map/dot_general | solution.py:127
  147.1 3.1 %fusion.25 = f32[128,256]{0,1:T(8,128)S(1)} fusion(bf16[256,120]{1,0:T(8,128)(2,1)S(1)} %copy-done.4, bf16[128,8192]{1,0:T(8,128)(2,1)} %all-gather.2.cloned.1.call-done, bf16[240,8192]{1,0:T(8,128)(2,1)} %param.11), kind=kOutput, calls=%fused_computation.32 | convolution fusion | flops 259537920 | bytes 4255744 | tf_op jit(solution)/shard_map/dot_general | solution.py:127
  151.8 1.6 copy.67
  154.3 12.1 %gather_fusion.1 = bf16[4096,128]{1,0:T(8,128)(2,1)S(1)} fusion(bf16[2048,128]{1,0:T(8,128)(2,1)S(1)} %bitcast.103, s32[4096]{0:T(1024)S(1)} %get-tuple-element.58), kind=kCustom, calls=%fused_computation.3 | custom fusion | bytes 2113536 | tf_op jit(solution)/shard_map/jit(_take)/gather | solution.py:72
  166.5 2.5 %select_select_fusion = bf16[32,128,128]{2,1,0:T(8,128)(2,1)} fusion(bf16[32,128,128]{2,1,0:T(8,128)(2,1)S(1)} %bitcast.104, pred[32,128]{1,0:T(8,128)(4,1)S(1)} %get-tuple-element.57, pred[32,128]{1,0:T(8,128)(4,1)S(1)} %iota_compare_fusion.12), kind=kLoop, calls=%fused_computation.35 | loop fusion | flops 1048576 | bytes 2105344 | tf_op jit(solution)/shard_map/jit(_where)/select_n | solution.py:71
  168.9 9.8 %all-to-all-start.1 = ((bf16[32,128,128]{2,1,0:T(8,128)(2,1)}), bf16[32,128,128]{2,1,0:T(8,128)(2,1)S(1)}, u32[]{:S(2)}, u32[]{:S(2)}) async-start(bf16[32,128,128]{2,1,0:T(8,128)(2,1)} %select_select_fusion), calls=%async_computation.2 | async-start | bytes 2097152 | tf_op jit(solution)/shard_map/all_to_all | solution.py:151
  179.2 0.7 reduce.3
  179.9 32.6 %all-to-all-done.1 = bf16[32,128,128]{2,1,0:T(8,128)(2,1)S(1)} async-done(((bf16[32,128,128]{2,1,0:T(8,128)(2,1)}), bf16[32,128,128]{2,1,0:T(8,128)(2,1)S(1)}, u32[]{:S(2)}, u32[]{:S(2)}) %all-to-all-start.1) | async-done | bytes 1048608 | tf_op jit(solution)/shard_map/all_to_all | solution.py:151
  212.5 3.8 %while.11 = (s32[]{:T(128)}, f32[512,128]{1,0:T(8,128)S(1)}, s32[4,1024]{1,0:T(4,128)S(1)}, bf16[4,1024,128]{2,1,0:T(8,128)(2,1)S(1)}, s32[]{:T(128)}, /*index=5*/s32[]{:T(128)}) while((s32[]{:T(128)}, f32[512,128]{1,0:T(8,128)S(1)}, s32[4,1024]{1,0:T(4,128)S(1)}, bf16[4,1024,128]{2,1,0:T(8,128)(2,1)S(1)}, s32[]{:T(128)}, ...), condition=%wide.region_9.11_spmd.clone, body=%wide.region_8.10_spmd.clone.sunk | while | flops 134873088 | bytes 798815 | solution.py:98
  212.5 0.9 fusion.73
  213.5 0.9 fusion.73
  214.4 0.9 fusion.73
  215.4 0.9 fusion.73
  216.3 2.6 %reduce-scatter.2.cloned.1.call-done = f32[240,256]{1,0:T(8,128)} async-done(((f32[240,8192]{1,0:T(8,128)}), f32[240,256]{1,0:T(8,128)}) %reduce-scatter.2.cloned.1.call-update) | async-done | bytes 245776 | tf_op jit(solution)/shard_map/reduce_scatter | solution.py:140
  218.9 1.6 convert_element_type.67
  (59 shorter events, 9.5 us)
Async XLA Ops:
  7.2 59.4 %all-gather.2.cloned.1.call-start = ((), (), s32[]{:S(2)}) async-start(), calls=%async_computation.3 | async-start | bytes 2359296 | tf_op jit(solution)/shard_map/all_gather | solution.py:111
  7.9 211.0 %reduce-scatter.2.cloned.1.call-start = ((), (), s32[]{:S(2)}) async-start(), calls=%async_computation.4 | async-start | bytes 8110080 | tf_op jit(solution)/shard_map/reduce_scatter | solution.py:140
  10.6 1.2 copy-start.1
  72.4 0.7 copy-start.2
  109.6 34.5 %copy-start = (bf16[128,8192]{1,0:T(8,128)(2,1)S(1)}, bf16[128,8192]{1,0:T(8,128)(2,1)}, u32[]{:S(2)}) copy-start(bf16[128,8192]{1,0:T(8,128)(2,1)} %all-gather.2.cloned.1.call-done) | copy-start | bytes 6291460
  109.6 34.5 %copy-start.4 = (bf16[256,120]{1,0:T(8,128)(2,1)S(1)}, bf16[256,120]{1,0:T(8,128)(2,1)}, u32[]{:S(2)}) copy-start(bf16[256,120]{1,0:T(8,128)(2,1)} %constant.88) | copy-start | bytes 184324
  133.3 35.6 %all-to-all-start = ((s32[32,128,1]{1,2,0:T(1,128)}), s32[32,128,1]{1,2,0:T(1,128)S(1)}, u32[]{:S(2)}, u32[]{:S(2)}) async-start(s32[32,128,1]{1,2,0:T(1,128)} %bitcast.19), calls=%async_computation.1 | async-start | bytes 32768 | tf_op jit(solution)/shard_map/all_to_all | solution.py:152
  168.9 43.5 %all-to-all-start.1 = ((bf16[32,128,128]{2,1,0:T(8,128)(2,1)}), bf16[32,128,128]{2,1,0:T(8,128)(2,1)S(1)}, u32[]{:S(2)}, u32[]{:S(2)}) async-start(bf16[32,128,128]{2,1,0:T(8,128)(2,1)} %select_select_fusion), calls=%async_computation.2 | async-start | bytes 2097152 | tf_op jit(solution)/shard_map/all_to_all | solution.py:151
  216.3 4.2 %copy-start.3 = (f32[512,128]{1,0:T(8,128)}, f32[512,128]{1,0:T(8,128)S(1)}, u32[]{:S(2)}) copy-start(f32[512,128]{1,0:T(8,128)S(1)} %get-tuple-element.29) | copy-start | bytes 786436
Sparse Core Ops, SparseCore 0:
  9.8 56.6 all-gather.1
  72.5 146.3 reduce-scatter.1
where the time goes:
time: 230 us; the launch traced here: 227 us
  waiting for transfers between devices  89.7 us (39%)
  local copies, waits for them, and re-layouts  77.5 us (34%)
  starting transfers between devices  20.5 us (9%)
  matrix products  18.2 us (8%)
  between operations  14.4 us (6%)
  other arithmetic  6.94 us (3%)
    all_gather x1, waiting for transfers between devices, on_device(): full_cotangent = lax.all_gather(cotangent, 'set', axis=1, tiled=True)  53.9 us
    all_to_all x1, waiting for transfers between devices, on_device(): lax.all_to_all(flat_values, 'dp', split_axis=0, concat_axis=0, tiled=True)  32.6 us
    gather x1, local copies, waits for them, and re-layouts, build_slots(): send_rows = jnp.where(is_live, jnp.take(compact_rows, source, axis=0), 0)  23 us
    gather x1, local copies, waits for them, and re-layouts, build_slots(): start_of = jnp.take_along_axis(before.T, chosen, axis=1)  17.4 us
    gather x1, local copies, waits for them, and re-layouts, build_slots(): jnp.take_along_axis(owner_start.astype(jnp.int32).T, chosen, axis=1)  17.4 us
    gather x1, local copies, waits for them, and re-layouts, build_slots(): jnp.take(compact_values, source, axis=0)  12.1 us
    all_to_all x1, starting transfers between devices, on_device(): lax.all_to_all(flat_slot_rows, 'dp', split_axis=0, concat_axis=0, tiled=T...  10.7 us
    all_to_all x1, starting transfers between devices, on_device(): lax.all_to_all(flat_values, 'dp', split_axis=0, concat_axis=0, tiled=True)  9.75 us
  transfers between devices with their start and end apart: 4, of which 3 were waited for; matrix products, arithmetic and copies ran while one was open for 42% of the time, Pallas kernels for 0%

commit v1 on v0

v1 whole, which is shorter than its diff:
```python
import functools

import jax
import jax.numpy as jnp
import numpy as np
from jax import lax
from jax.experimental import pallas as pl
from jax.experimental.pallas import tpu as pltpu
from jax.sharding import PartitionSpec as P

K = 64
F = 16
ROWS_DEV = 512
PAIRS = 120
B = 128
KEEP = 62
XROWS = 80
DP = 32
BF = jnp.bfloat16
F32 = jnp.float32
MESH = pl.DeviceIdType.MESH


def constants():
    first, second = np.triu_indices(F, 1)
    spread = np.zeros((256, F, 16), np.float32)
    mask = np.zeros((F, 16, 256), np.float32)
    for p in range(PAIRS):
        spread[p, second[p], :] = 1
        spread[128 + p, first[p], :] = 1
        mask[first[p], :, p] = 1
        mask[second[p], :, 128 + p] = 1
    spread = spread.reshape(256, 256)
    pick = np.ascontiguousarray(spread[:128].T)
    return [a.astype(BF) for a in (spread, pick, mask.reshape(256, 256))]


def dot(a, b):
    return jnp.dot(a, b, preferred_element_type=F32)


def dot_nt(a, b):
    return lax.dot_general(a, b, (((1,), (1,)), ((), ())), preferred_element_type=F32)


def kernel(emb_ref, cot_ref, w_ref, rows_ref, spread_ref, pick_ref, mask_ref, wg_ref, tg_ref,
           cot_v, sib_v, w_v, ei, items, pairs_v, pt_v, pg_v, rowpad, pos_v, vals_v, meta_v,
           hot_v, hotx_v, rs_s, rs_r, y_s, y_r, send_v, recv_v, x_s, x_r,
           loc_sem, ag_ss, ag_rs, sib_ss, sib_rs, pt_ss, pt_rs, rs_ss, rs_rs, y_ss, y_rs,
           a_ss, a_rs, x_ss, x_rs):
    me_s = lax.axis_index("set")
    me_d = lax.axis_index("dp")
    x, yl = me_s // 2, me_s % 2
    right = ((x + 1) % 4) * 2 + yl
    left = ((x + 3) % 4) * 2 + yl
    opp = ((x + 2) % 4) * 2 + yl
    over = me_s + 1 - 2 * yl
    right_o = right + 1 - 2 * yl
    left_o = left + 1 - 2 * yl
    opp_o = opp + 1 - 2 * yl
    z, yh, core = me_d // 4, (me_d // 2) % 2, me_d % 2
    twin = me_d + 1 - 2 * core
    y_part = me_d + 2 - 4 * yh
    z_up, z_down = (me_d + 4) % DP, (me_d + 28) % DP

    def rcopy(src, dst, ss, rs, **where):
        return pltpu.make_async_remote_copy(
            src_ref=src, dst_ref=dst, send_sem=ss, recv_sem=rs, device_id=where, device_id_type=MESH)

    own_copies = []
    for h in range(2):
        for cc in range(2):
            own_copies.append(pltpu.make_async_copy(
                cot_ref.at[:, pl.ds((h * 2 + cc) * 256, 256)], cot_v.at[me_s, cc, h], loc_sem.at[h * 2 + cc]))
    w_copy = pltpu.make_async_copy(w_ref, w_v, loc_sem.at[4])
    for copy in own_copies:
        copy.start()
    w_copy.start()

    barrier = pltpu.get_barrier_semaphore()
    for peer in (right, left, over):
        pl.semaphore_signal(barrier, inc=1, device_id={"set": peer}, device_id_type=MESH)

    def greet(i, carry):
        pl.semaphore_signal(barrier, inc=1, device_id={"dp": (me_d + i) % DP}, device_id_type=MESH)
        return carry

    lax.fori_loop(1, DP, greet, 0)
    for copy in own_copies:
        copy.wait()
    pl.semaphore_wait(barrier, 3 + DP - 1)

    def ag(k, src, peer):
        return rcopy(src, src, ag_ss.at[k], ag_rs.at[k], set=peer)

    def ag_wait(k, block):
        rcopy(block, block, ag_ss.at[k], ag_rs.at[k], set=right).wait_recv()

    sent = []

    def start(copy):
        copy.start()
        sent.append(copy)

    start(ag(0, cot_v.at[me_s], right))
    start(ag(1, cot_v.at[me_s], left))
    start(ag(2, cot_v.at[me_s], over))

    def to_twin(t, j):
        start(rcopy(cot_v.at[j, 1 - core], sib_v.at[j], sib_ss.at[t], sib_rs.at[t], dp=twin))

    to_twin(0, me_s)

    lane = lax.broadcasted_iota(jnp.int32, (B, 128), 1)
    for m in range(8):
        a = emb_ref[0, :, m * 128:(m + 1) * 128].astype(F32)
        b = emb_ref[1, :, m * 128:(m + 1) * 128].astype(F32)
        ei[2 * m] = jnp.where(lane < 64, a, pltpu.roll(b, 64, 1)).astype(BF)
        ei[2 * m + 1] = jnp.where(lane < 64, pltpu.roll(a, 64, 1), b).astype(BF)

    def diagonal():
        r = lax.broadcasted_iota(jnp.int32, (256, 256), 0)
        c = lax.broadcasted_iota(jnp.int32, (256, 256), 1)
        return (r % 16) == (c % 16)

    def group_rows(g):
        return pl.ds(pl.multiple_of(g * 16, 16), 16)

    def pair_step(g, carry):
        eg = ei[:, group_rows(g), :].reshape(256, 128)
        lane_g = lax.broadcasted_iota(jnp.int32, (256, 128), 1)
        for s in range(2):
            half = jnp.where((lane_g < 64) == (s == 0), eg.astype(F32), 0.0).astype(BF)
            gram = jnp.where(diagonal(), dot_nt(half, eg), 0.0).astype(BF)
            picked = dot(gram, pick_ref[...]) * mask_ref[:, :128].astype(F32)
            pairs_v[group_rows(g), s * 128:(s + 1) * 128] = jnp.sum(picked.reshape(F, 16, 128), axis=0)
        return carry

    lax.fori_loop(0, B // 16, pair_step, 0)
    turned = pairs_v[...].T
    pt_v[:, :B] = jnp.concatenate([turned[:PAIRS], turned[128:128 + PAIRS]], axis=0).astype(BF)
    start(rcopy(pt_v.at[:, pl.ds(0, B)], pt_v.at[:, pl.ds(B, B)], pt_ss, pt_rs, dp=twin))

    w_copy.wait()
    pg_v[...] = jnp.zeros_like(pg_v)

    def pg_add(j):
        total = None
        for h in range(2):
            for cc in range(2):
                cols = pl.ds(pl.multiple_of(j * 1024 + (h * 2 + cc) * 256, 256), 256)
                part = dot_nt(cot_v[j, cc, h], w_v[:, cols])
                total = part if total is None else total + part
        pg_v[:, :2 * PAIRS] += total

    pg_add(me_s)

    rowpad[...] = jnp.zeros_like(rowpad)
    rowpad[:, :F] = rows_ref[...].astype(F32)
    rows_t = rowpad[...].T[:F]
    owner = jnp.floor(rows_t * (1.0 / ROWS_DEV))
    local = rows_t - owner * ROWS_DEV
    local_hi = jnp.floor(local * (1.0 / 256))
    g_hi = jnp.floor(rows_t * (1.0 / 128))
    before = (lax.broadcasted_iota(jnp.int32, (128, 128), 0)
              < lax.broadcasted_iota(jnp.int32, (128, 128), 1)).astype(F32).astype(BF)
    owner_id = lax.broadcasted_iota(jnp.int32, (DP, 128), 0).astype(F32)
    seen = jnp.zeros((DP, 1), F32)
    vals_v[...] = jnp.zeros_like(vals_v)
    for f in range(F):
        hot = jnp.where(owner_id == owner[f:f + 1], 1.0, 0.0)
        earlier = dot(hot.astype(BF), before) + seen
        seen = seen + jnp.sum(hot, axis=1, keepdims=True)
        rank = jnp.sum(hot * earlier, axis=0, keepdims=True)
        pos = jnp.where(rank < KEEP, owner[f:f + 1] * 64 + rank, DP * 64 + rank - KEEP)
        pos_v[f:f + 1, :] = pos.astype(jnp.int32)
        cols = slice(f * 128, (f + 1) * 128)
        vals_v[0:1, cols] = local[f:f + 1] - 256 * local_hi[f:f + 1]
        vals_v[1:2, cols] = local_hi[f:f + 1]
        vals_v[2:3, cols] = rows_t[f:f + 1] - 128 * g_hi[f:f + 1]
        vals_v[3:4, cols] = g_hi[f:f + 1]

    def hot_step(k, carry):
        slot = lax.broadcasted_iota(jnp.int32, (256, 128), 0) + k * 256
        for f in range(F):
            hot_v[k, :, f * 128:(f + 1) * 128] = jnp.where(slot == pos_v[f:f + 1, :], 1.0, 0.0).astype(BF)
        ids = dot_nt(vals_v[...].astype(BF), hot_v[k])
        low = lax.broadcasted_iota(jnp.int32, (1, 128), 1) < 64
        for q in range(4):
            cols = slice((q // 2) * 128, (q // 2) * 128 + 128)
            lo, hi = ids[0:1, cols], ids[1:2, cols]
            if q % 2 == 0:
                row = jnp.where(low, lo, pltpu.roll(jnp.broadcast_to(hi, (8, 128)), 64, 1)[0:1])
            else:
                row = jnp.where(low, pltpu.roll(jnp.broadcast_to(lo, (8, 128)), 64, 1)[0:1], hi)
            meta_v[k, q:q + 1, :] = row
        return carry

    ag_wait(0, cot_v.at[left])
    start(ag(5, cot_v.at[left, 0], right))
    ag_wait(1, cot_v.at[right])
    start(ag(6, cot_v.at[right, 1], left))
    ag_wait(2, cot_v.at[over])
    start(ag(3, cot_v.at[over], right))
    start(ag(4, cot_v.at[over], left))
    to_twin(1, left)
    to_twin(2, right)
    to_twin(3, over)
    pg_add(left)
    pg_add(right)
    pg_add(over)
    lax.fori_loop(0, 4, hot_step, 0)

    ag_wait(5, cot_v.at[opp, 0])
    start(ag(7, cot_v.at[opp, 0], over))
    ag_wait(6, cot_v.at[opp, 1])
    start(ag(8, cot_v.at[opp, 1], over))
    to_twin(4, opp)
    pg_add(opp)
    lax.fori_loop(4, 8, hot_step, 0)
    slot_x = lax.broadcasted_iota(jnp.int32, (XROWS, 128), 0) + DP * 64
    for f in range(F):
        hotx_v[:, f * 128:(f + 1) * 128] = jnp.where(slot_x == pos_v[f:f + 1, :], 1.0, 0.0).astype(BF)
    ids_x = dot_nt(vals_v[...].astype(BF), hotx_v[...])

    ag_wait(3, cot_v.at[left_o])
    ag_wait(4, cot_v.at[right_o])
    to_twin(5, left_o)
    to_twin(6, right_o)
    pg_add(left_o)
    pg_add(right_o)
    ag_wait(7, cot_v.at[opp_o, 0])
    ag_wait(8, cot_v.at[opp_o, 1])
    to_twin(7, opp_o)
    pg_add(opp_o)

    rcopy(pt_v.at[:, pl.ds(0, B)], pt_v.at[:, pl.ds(B, B)], pt_ss, pt_rs, dp=twin).wait_recv()
    for t, j in enumerate((me_s, left, right, over, opp, left_o, right_o, opp_o)):
        rcopy(cot_v.at[j, 1 - core], sib_v.at[j], sib_ss.at[t], sib_rs.at[t], dp=twin).wait_recv()

    def part(j, h):
        return dot(pt_v[...], jnp.concatenate([cot_v[j, core, h], sib_v[j, h]], axis=0))

    def rs_copy(way, k, h):
        return rcopy(rs_s.at[way, k, h], rs_r.at[way, k, h], rs_ss.at[way, k, h], rs_rs.at[way, k, h],
                     dp=z_up if way else z_down)

    def rs_step(way, k, h):
        j = (z + 12 - k) % 8 if way else (z + 4 + k) % 8
        value = part(j, h)
        if k >= 2 or (k == 1 and h == way):
            rs_copy(way, k - 1, h).wait_recv()
            value = value + rs_r[way, k - 1, h].astype(F32)
        rs_s[way, k, h] = value.astype(BF)
        start(rs_copy(way, k, h))

    rs_step(0, 0, 0)
    rs_step(1, 0, 1)
    rs_step(0, 1, 1)
    rs_step(1, 1, 0)

    pg_all = pg_v[...]
    pg_v[...] = pg_all.astype(BF).astype(F32)

    def emb_step(g, carry):
        eg = ei[:, group_rows(g), :].reshape(256, 128)
        a = pg_v[group_rows(g), :]
        grads = []
        for s in range(2):
            one = (a if s == 0 else pltpu.roll(a, 256 - PAIRS, 1))[:, :128]
            both = jnp.concatenate([one, one], axis=1).astype(BF)
            tall = jnp.concatenate([both] * F, axis=0) * mask_ref[...]
            sym = jnp.where(diagonal(), dot(tall, spread_ref[...]), 0.0).astype(BF)
            grads.append(dot(sym, eg))
        lane_g = lax.broadcasted_iota(jnp.int32, (256, 128), 1)
        items[:, group_rows(g), :] = jnp.where(lane_g < 64, grads[0], grads[1]).astype(BF).reshape(F, 16, 128)
        return carry

    lax.fori_loop(0, B // 16, emb_step, 0)

    rs_step(0, 1, 0)
    rs_step(1, 1, 1)

    def x_copy(i):
        return rcopy(x_s, x_r.at[me_d], x_ss.at[i], x_rs.at[me_d], dp=(me_d + i) % DP)

    x_tile = dot(hotx_v[...], items[...].reshape(B * F, 128))
    row_x = lax.broadcasted_iota(jnp.int32, (XROWS, 128), 0)
    ids_x = jnp.concatenate([ids_x, jnp.zeros((ids_x.shape[0], 128 - XROWS), F32)], axis=1)
    x_tile = jnp.where(row_x == 66, ids_x[2:3], jnp.where(row_x == 67, ids_x[3:4], x_tile))
    x_s[...] = x_tile.astype(BF)
    x_r[me_d] = x_tile.astype(BF)

    def x_start(i, carry):
        x_copy(i).start()
        return carry

    lax.fori_loop(1, DP, x_start, 0)

    def a_copy(o):
        return rcopy(send_v.at[o], recv_v.at[me_d], a_ss.at[o], a_rs.at[me_d], dp=o)

    def a_step(i, carry):
        k = (z + 4 + i) % 8
        tile = dot(hot_v[k], items[...].reshape(B * F, 128))
        row = lax.broadcasted_iota(jnp.int32, (64, 128), 0)
        for q in range(4):
            o = k * 4 + q
            block = jnp.where(row == KEEP, meta_v[k, q:q + 1, :], tile[q * 64:(q + 1) * 64]).astype(BF)
            send_v[o] = block

            @pl.when(o == me_d)
            def _():
                recv_v[o] = block

            @pl.when(o != me_d)
            def _():
                a_copy(o).start()
        return carry

    lax.fori_loop(0, 4, a_step, 0)
    for way in range(2):
        rs_step(way, 2, 0)
        rs_step(way, 2, 1)
    lax.fori_loop(4, 8, a_step, 0)
    for way in range(2):
        rs_step(way, 3, 0)
        rs_step(way, 3, 1)

    tg_ref[...] = jnp.zeros_like(tg_ref)
    row_id = lax.broadcasted_iota(jnp.int32, (ROWS_DEV, 128), 0).astype(F32)

    def a_add(i, carry):
        k = (z + 8 - i) % 8
        low = lax.broadcasted_iota(jnp.int32, (8, 128), 1) < 64
        dead = lax.broadcasted_iota(jnp.int32, (8, 128), 1) % 64 >= KEEP
        for q in range(4):
            @pl.when(k * 4 + q != me_d)
            def _():
                rcopy(send_v.at[me_d], recv_v.at[k * 4 + q], a_ss.at[me_d], a_rs.at[k * 4 + q], dp=twin).wait_recv()
        ids = []
        for q in range(4):
            got = jnp.broadcast_to(recv_v[k * 4 + q, KEEP:KEEP + 1, :].astype(F32), (8, 128))
            turn = pltpu.roll(got, 64, 1)
            ids.append(got + 256 * turn if q % 2 == 0 else turn + 256 * got)
        hots = []
        for m in range(2):
            both = jnp.where(dead, -1.0, jnp.where(low, ids[2 * m], ids[2 * m + 1]))[0:1]
            hots.append(jnp.where(row_id == both, 1.0, 0.0).astype(BF))
        values = recv_v[pl.ds(pl.multiple_of(k * 4, 4), 4)].reshape(256, 128)
        tg_ref[...] += dot(jnp.concatenate(hots, axis=1), values)
        return carry

    lax.fori_loop(0, 8, a_add, 0)

    for way in range(2):
        for h in range(2):
            rs_copy(way, 3, h).wait_recv()

    def whole(h):
        return part(z, h) + rs_r[0, 3, h].astype(F32) + rs_r[1, 3, h].astype(F32)

    y_s[...] = whole(1 - yh).astype(BF)
    y_copy = rcopy(y_s, y_r, y_ss, y_rs, dp=y_part)
    y_copy.start()

    base = (me_d * ROWS_DEV).astype(F32)

    def x_add(i, carry):
        src = (me_d + i) % DP

        @pl.when(src != me_d)
        def _():
            rcopy(x_s, x_r.at[src], x_ss.at[0], x_rs.at[src], dp=twin).wait_recv()

        low = x_r[src, 66:67, :].astype(F32)
        high = x_r[src, 67:68, :].astype(F32)
        ids = low + 128 * high - base
        ids = jnp.where(lax.broadcasted_iota(jnp.int32, (1, 128), 1) < 66, ids, -1.0)
        hot = jnp.where(row_id == ids, 1.0, 0.0).astype(BF)
        tg_ref[...] += dot(hot[:, :XROWS], x_r[src])
        return carry

    lax.fori_loop(0, DP, x_add, 0)

    last = whole(yh)
    y_copy.wait()
    wg_ref[...] = (last + y_r[...].astype(F32)).astype(BF)

    for copy in sent:
        copy.wait_send()

    def drain(i, carry):
        x_copy(i).wait_send()
        a_copy((me_d + i) % DP).wait_send()
        return carry

    lax.fori_loop(1, DP, drain, 0)


def on_device(embeddings, cotangent, first_weight, feature_rows):
    vmem = pl.BlockSpec(memory_space=pltpu.VMEM)
    hbm = pl.BlockSpec(memory_space=pl.ANY)
    dma = pltpu.SemaphoreType.DMA
    consts = [jnp.asarray(a) for a in constants()]
    return pl.pallas_call(
        kernel,
        out_shape=(jax.ShapeDtypeStruct((2 * PAIRS, 256), BF), jax.ShapeDtypeStruct((ROWS_DEV, 128), F32)),
        in_specs=[vmem, hbm, hbm, vmem, vmem, vmem, vmem],
        out_specs=(vmem, vmem),
        scratch_shapes=[
            pltpu.VMEM((8, 2, 2, B, 256), BF),
            pltpu.VMEM((8, 2, B, 256), BF),
            pltpu.VMEM((2 * PAIRS, 8192), BF),
            pltpu.VMEM((F, B, 128), BF),
            pltpu.VMEM((F, B, 128), BF),
            pltpu.VMEM((B, 256), F32),
            pltpu.VMEM((2 * PAIRS, 256), BF),
            pltpu.VMEM((B, 256), F32),
            pltpu.VMEM((B, 128), F32),
            pltpu.VMEM((F, 128), jnp.int32),
            pltpu.VMEM((16, B * F), F32),
            pltpu.VMEM((8, 8, 128), F32),
            pltpu.VMEM((8, 256, B * F), BF),
            pltpu.VMEM((XROWS, B * F), BF),
            pltpu.VMEM((2, 4, 2, 2 * PAIRS, 256), BF),
            pltpu.VMEM((2, 4, 2, 2 * PAIRS, 256), BF),
            pltpu.VMEM((2 * PAIRS, 256), BF),
            pltpu.VMEM((2 * PAIRS, 256), BF),
            pltpu.VMEM((DP, 64, 128), BF),
            pltpu.VMEM((DP, 64, 128), BF),
            pltpu.VMEM((XROWS, 128), BF),
            pltpu.VMEM((DP, XROWS, 128), BF),
            dma((5,)), dma((9,)), dma((9,)), dma((8,)), dma((8,)), dma, dma,
            dma((2, 4, 2)), dma((2, 4, 2)), dma, dma,
            dma((DP,)), dma((DP,)), dma((DP,)), dma((DP,)),
        ],
        compiler_params=pltpu.CompilerParams(
            collective_id=0, has_side_effects=True, vmem_limit_bytes=56 * 1024 * 1024),
    )(embeddings, cotangent, first_weight, feature_rows, *consts)


def solution(mesh):
    return jax.shard_map(
        on_device,
        mesh=mesh,
        in_specs=(P("set", "dp", None), P("dp", "set"), P("set", None), P("dp", None)),
        out_specs=(P("set", "dp"), P("dp", "set")),
        check_vma=False,
    )
```

time: 230 us -> 96.4 us (0.42); the launches traced: 227 us -> 96.3 us
  Pallas kernels: 0 us -> 91 us
  waiting for transfers between devices: 89.7 us -> 0 us
  local copies, waits for them, and re-layouts: 77.5 us -> 4.65 us
  starting transfers between devices: 20.5 us -> 0 us
  matrix products: 18.2 us -> 0 us
  between operations: 14.4 us -> 0.64 us
  other arithmetic: 6.94 us -> 0 us
    pallas_call x0 -> x1, Pallas kernels: none -> 91 us  [on_device(): pl.pallas_call(kernel, out_shape=(jax.ShapeDtypeStruct((2 * PAIRS, 256),...]
    gather x4 -> x0, local copies, waits for them, and re-layouts: 70 us -> none  [the longest x1 23 us: build_slots(): send_rows = jnp.where(is_live, jnp.take(compact_rows, source, axis=0), 0)]
    all_gather x1 -> x0, waiting for transfers between devices: 53.9 us -> none  [on_device(): full_cotangent = lax.all_gather(cotangent, 'set', axis=1, tiled=True)]
    all_to_all x2 -> x0, waiting for transfers between devices: 32.6 us -> none  [the longest x1 32.6 us: on_device(): lax.all_to_all(flat_values, 'dp', split_axis=0, concat_axis=0, tiled=True)]
    all_to_all x2 -> x0, starting transfers between devices: 20.5 us -> none  [the longest x1 10.7 us: on_device(): lax.all_to_all(flat_slot_rows, 'dp', split_axis=0, concat_axis=0, tiled=T...]
    dot_general x15 -> x0, matrix products: 18.2 us -> none  [the longest x1 5.85 us: on_device(): lax.dot_general(pairs_all, full_cotangent, (((0,), (0,)), ((), ())), pref...]
    unnamed x14 -> x3, local copies, waits for them, and re-layouts: 1.13 us -> 4.65 us
    select_n x3 -> x0, other arithmetic: 3.16 us -> none  [the longest x1 2.47 us: build_slots(): jnp.where(is_live[:, :, None], jnp.take(compact_values, source, axis=0),...]
  transfers between devices with their start and end apart: 4 -> 0, of which waited for: 3 -> 0; matrix products, arithmetic and copies ran while one was open for 42% -> 0% of each run, Pallas kernels for 0% -> 0%
where the time goes in v1:
time: 96.4 us; the launch traced here: 96.3 us
  Pallas kernels  91 us (94%)
  local copies, waits for them, and re-layouts  4.65 us (5%)
    pallas_call x1, Pallas kernels, on_device(): pl.pallas_call(kernel, out_shape=(jax.ShapeDtypeStruct((2 * PAIRS, 256),...  91 us
    unnamed x3, local copies, waits for them, and re-layouts  4.65 us

profile of v1, /device:TPU:1, one launch (start us, length us, event | category | flops | bytes accessed | tf_op | source)
XLA Modules:
  0.0 96.3 jit_solution(6819239989299833026)
XLA Ops:
  0.6 1.4 %copy.9.rows_ref = s32[128,16]{1,0:T(8,128)} copy(s32[128,16]{0,1:T(8,128)} %param.10) | data formatting | bytes 16384 | tf_op args[3]
  2.1 91.0 %shard_map.86 = (bf16[240,256]{1,0:T(8,128)(2,1)}, f32[512,128]{1,0:T(8,128)}) custom-call(bf16[2,128,1024]{2,1,0:T(8,128)(2,1)} %emb_ref.1, bf16[128,1024]{1,0:T(8,128)(2,1)} %cot_ref.1, bf16[240,8192]{1,0:T(8,128)(2,1)} %w_ref.1, s32[128,16]{1,0:T(8,128)} %copy.9.rows_ref, bf16[256,256]{1,0:T(8,128)(2,1)} %constant.6.clone.spread_ref, ...), custom_call_target="tpu_custom_call" | custom-call | tf_op jit(solution)/shard_map/pallas_call | solution.py:406
  93.0 1.6 %copy.12 = bf16[240,256]{1,0:T(8,128)(2,1)} copy(bf16[240,256]{1,0:T(8,128)(2,1)} %get-tuple-element.4) | data formatting | bytes 245760
  94.6 1.7 %copy.13 = f32[512,128]{1,0:T(8,128)} copy(f32[512,128]{1,0:T(8,128)} %get-tuple-element.5) | data formatting | bytes 524288

commit v2 on v1

--- a/solution.py
+++ b/solution.py
@@ -43,9 +43,10 @@
     return lax.dot_general(a, b, (((1,), (1,)), ((), ())), preferred_element_type=F32)
 
 
-def kernel(emb_ref, cot_ref, w_ref, rows_ref, spread_ref, pick_ref, mask_ref, wg_ref, tg_ref,
-           cot_v, sib_v, w_v, ei, items, pairs_v, pt_v, pg_v, rowpad, pos_v, vals_v, meta_v,
-           hot_v, hotx_v, rs_s, rs_r, y_s, y_r, send_v, recv_v, x_s, x_r,
+def kernel(emb_hbm, cot_ref, w_ref, rows_ref, spread_hbm, pick_hbm, mask_hbm, wg_ref, tg_ref,
+           emb_ref, spread_ref, pick_ref, mask_ref,
+           cot_v, sib_v, w_v, ei, items, pairs_v, pt_v, pg_v, pos_v, vals_v, meta_v,
+           hot_v, hotx_v, rs_s, rs_r, y_s, y_r, send_v, recv_v, x_v,
            loc_sem, ag_ss, ag_rs, sib_ss, sib_rs, pt_ss, pt_rs, rs_ss, rs_rs, y_ss, y_rs,
            a_ss, a_rs, x_ss, x_rs):
     me_s = lax.axis_index("set")
@@ -72,10 +73,10 @@
         for cc in range(2):
             own_copies.append(pltpu.make_async_copy(
                 cot_ref.at[:, pl.ds((h * 2 + cc) * 256, 256)], cot_v.at[me_s, cc, h], loc_sem.at[h * 2 + cc]))
-    w_copy = pltpu.make_async_copy(w_ref, w_v, loc_sem.at[4])
-    for copy in own_copies:
+    inputs = ((emb_hbm, emb_ref), (pick_hbm, pick_ref), (mask_hbm, mask_ref), (spread_hbm, spread_ref), (w_ref, w_v))
+    in_copies = [pltpu.make_async_copy(a, b, loc_sem.at[4 + i]) for i, (a, b) in enumerate(inputs)]
+    for copy in own_copies + in_copies:
         copy.start()
-    w_copy.start()
 
     barrier = pltpu.get_barrier_semaphore()
     for peer in (right, left, over):
@@ -90,27 +91,34 @@
         copy.wait()
     pl.semaphore_wait(barrier, 3 + DP - 1)
 
-    def ag(k, src, peer):
-        return rcopy(src, src, ag_ss.at[k], ag_rs.at[k], set=peer)
-
-    def ag_wait(k, block):
-        rcopy(block, block, ag_ss.at[k], ag_rs.at[k], set=right).wait_recv()
-
     sent = []
 
     def start(copy):
         copy.start()
         sent.append(copy)
 
-    start(ag(0, cot_v.at[me_s], right))
-    start(ag(1, cot_v.at[me_s], left))
-    start(ag(2, cot_v.at[me_s], over))
+    def ag(k, src, peer):
+        start(rcopy(src, src, ag_ss.at[k], ag_rs.at[k], set=peer))
+
+    def ag_wait(k, block):
+        rcopy(block, block, ag_ss.at[k], ag_rs.at[k], set=right).wait_recv()
+
+    ag(0, cot_v.at[me_s, 0], right)
+    ag(2, cot_v.at[me_s, 1], left)
+    ag(4, cot_v.at[me_s], over)
+    ag(1, cot_v.at[me_s, 1], right)
+    ag(3, cot_v.at[me_s, 0], left)
+
+    def twin_copy(t, j):
+        return rcopy(cot_v.at[j, 1 - core], sib_v.at[j], sib_ss.at[t], sib_rs.at[t], dp=twin)
 
     def to_twin(t, j):
-        start(rcopy(cot_v.at[j, 1 - core], sib_v.at[j], sib_ss.at[t], sib_rs.at[t], dp=twin))
+        start(twin_copy(t, j))
 
     to_twin(0, me_s)
 
+    for copy in in_copies[:4]:
+        copy.wait()
     lane = lax.broadcasted_iota(jnp.int32, (B, 128), 1)
     for m in range(8):
         a = emb_ref[0, :, m * 128:(m + 1) * 128].astype(F32)
@@ -136,12 +144,29 @@
             pairs_v[group_rows(g), s * 128:(s + 1) * 128] = jnp.sum(picked.reshape(F, 16, 128), axis=0)
         return carry
 
-    lax.fori_loop(0, B // 16, pair_step, 0)
+    lax.fori_loop(0, 4, pair_step, 0)
+
+    ag_wait(0, cot_v.at[left, 0])
+    ag(5, cot_v.at[left, 0], right)
+    ag_wait(2, cot_v.at[right, 1])
+    ag(6, cot_v.at[right, 1], left)
+
+    lax.fori_loop(4, 8, pair_step, 0)
     turned = pairs_v[...].T
     pt_v[:, :B] = jnp.concatenate([turned[:PAIRS], turned[128:128 + PAIRS]], axis=0).astype(BF)
-    start(rcopy(pt_v.at[:, pl.ds(0, B)], pt_v.at[:, pl.ds(B, B)], pt_ss, pt_rs, dp=twin))
-
-    w_copy.wait()
+    pt_copy = rcopy(pt_v.at[:, pl.ds(0, B)], pt_v.at[:, pl.ds(B, B)], pt_ss, pt_rs, dp=twin)
+    start(pt_copy)
+
+    ag_wait(4, cot_v.at[over])
+    ag(7, cot_v.at[over], right)
+    ag(8, cot_v.at[over], left)
+    to_twin(1, over)
+    ag_wait(1, cot_v.at[left, 1])
+    ag_wait(3, cot_v.at[right, 0])
+    to_twin(2, left)
+    to_twin(3, right)
+
+    in_copies[4].wait()
     pg_v[...] = jnp.zeros_like(pg_v)
 
     def pg_add(j):
@@ -149,15 +174,48 @@
         for h in range(2):
             for cc in range(2):
                 cols = pl.ds(pl.multiple_of(j * 1024 + (h * 2 + cc) * 256, 256), 256)
-                part = dot_nt(cot_v[j, cc, h], w_v[:, cols])
-                total = part if total is None else total + part
+                term = dot_nt(cot_v[j, cc, h], w_v[:, cols])
+                total = term if total is None else total + term
         pg_v[:, :2 * PAIRS] += total
 
-    pg_add(me_s)
-
-    rowpad[...] = jnp.zeros_like(rowpad)
-    rowpad[:, :F] = rows_ref[...].astype(F32)
-    rows_t = rowpad[...].T[:F]
+    def part(j, h):
+        return dot(pt_v[...], jnp.concatenate([cot_v[j, core, h], sib_v[j, h]], axis=0))
+
+    def rs_copy(way, k, h):
+        return rcopy(rs_s.at[way, k, h], rs_r.at[way, k, h], rs_ss.at[way, k, h], rs_rs.at[way, k, h],
+                     dp=z_up if way else z_down)
+
+    def rs_step(late, way, k, h):
+        j = (z + 12 - k) % 8 if way else (z + 4 + k) % 8
+        is_late = (j == left_o) | (j == right_o) | (j == opp_o)
+
+        @pl.when(is_late if late else jnp.logical_not(is_late))
+        def _():
+            value = part(j, h)
+            if k >= 2 or (k == 1 and h == way):
+                rs_copy(way, k - 1, h).wait_recv()
+                value = value + rs_r[way, k - 1, h].astype(F32)
+            rs_s[way, k, h] = value.astype(BF)
+            rs_copy(way, k, h).start()
+
+    def rs_round(late, n):
+        for way in range(2):
+            if n < 4:
+                rs_step(late, way, n, way)
+        for way in range(2):
+            if n < 3:
+                rs_step(late, way, n + 1, 1 - way)
+
+    for j in (me_s, over, left, right):
+        pg_add(j)
+
+    ag_wait(5, cot_v.at[opp, 0])
+    ag(9, cot_v.at[opp, 0], over)
+    ag_wait(6, cot_v.at[opp, 1])
+    ag(10, cot_v.at[opp, 1], over)
+    to_twin(4, opp)
+
+    rows_t = rows_ref[...].astype(F32)
     owner = jnp.floor(rows_t * (1.0 / ROWS_DEV))
     local = rows_t - owner * ROWS_DEV
     local_hi = jnp.floor(local * (1.0 / 256))
@@ -196,68 +254,29 @@
             meta_v[k, q:q + 1, :] = row
         return carry
 
-    ag_wait(0, cot_v.at[left])
-    start(ag(5, cot_v.at[left, 0], right))
-    ag_wait(1, cot_v.at[right])
-    start(ag(6, cot_v.at[right, 1], left))
-    ag_wait(2, cot_v.at[over])
-    start(ag(3, cot_v.at[over], right))
-    start(ag(4, cot_v.at[over], left))
-    to_twin(1, left)
-    to_twin(2, right)
-    to_twin(3, over)
-    pg_add(left)
-    pg_add(right)
-    pg_add(over)
-    lax.fori_loop(0, 4, hot_step, 0)
-
-    ag_wait(5, cot_v.at[opp, 0])
-    start(ag(7, cot_v.at[opp, 0], over))
-    ag_wait(6, cot_v.at[opp, 1])
-    start(ag(8, cot_v.at[opp, 1], over))
-    to_twin(4, opp)
+    pt_copy.wait_recv()
+    for t, j in enumerate((me_s, over, left, right, opp)):
+        twin_copy(t, j).wait_recv()
+    rs_round(False, 0)
     pg_add(opp)
-    lax.fori_loop(4, 8, hot_step, 0)
+    lax.fori_loop(0, 8, hot_step, 0)
     slot_x = lax.broadcasted_iota(jnp.int32, (XROWS, 128), 0) + DP * 64
     for f in range(F):
         hotx_v[:, f * 128:(f + 1) * 128] = jnp.where(slot_x == pos_v[f:f + 1, :], 1.0, 0.0).astype(BF)
     ids_x = dot_nt(vals_v[...].astype(BF), hotx_v[...])
-
-    ag_wait(3, cot_v.at[left_o])
-    ag_wait(4, cot_v.at[right_o])
-    to_twin(5, left_o)
-    to_twin(6, right_o)
+    x_v[:, :, :, XROWS:] = jnp.zeros((2, 2, 8, 128 - XROWS, 128), BF)
+    rs_round(False, 1)
+
+    ag_wait(9, cot_v.at[opp_o, 0])
+    ag_wait(10, cot_v.at[opp_o, 1])
+    to_twin(5, opp_o)
+    pg_add(opp_o)
+    ag_wait(7, cot_v.at[left_o])
+    to_twin(6, left_o)
+    ag_wait(8, cot_v.at[right_o])
+    to_twin(7, right_o)
     pg_add(left_o)
     pg_add(right_o)
-    ag_wait(7, cot_v.at[opp_o, 0])
-    ag_wait(8, cot_v.at[opp_o, 1])
-    to_twin(7, opp_o)
-    pg_add(opp_o)
-
-    rcopy(pt_v.at[:, pl.ds(0, B)], pt_v.at[:, pl.ds(B, B)], pt_ss, pt_rs, dp=twin).wait_recv()
-    for t, j in enumerate((me_s, left, right, over, opp, left_o, right_o, opp_o)):
-        rcopy(cot_v.at[j, 1 - core], sib_v.at[j], sib_ss.at[t], sib_rs.at[t], dp=twin).wait_recv()
-
-    def part(j, h):
-        return dot(pt_v[...], jnp.concatenate([cot_v[j, core, h], sib_v[j, h]], axis=0))
-
-    def rs_copy(way, k, h):
-        return rcopy(rs_s.at[way, k, h], rs_r.at[way, k, h], rs_ss.at[way, k, h], rs_rs.at[way, k, h],
-                     dp=z_up if way else z_down)
-
-    def rs_step(way, k, h):
-        j = (z + 12 - k) % 8 if way else (z + 4 + k) % 8
-        value = part(j, h)
-        if k >= 2 or (k == 1 and h == way):
-            rs_copy(way, k - 1, h).wait_recv()
-            value = value + rs_r[way, k - 1, h].astype(F32)
-        rs_s[way, k, h] = value.astype(BF)
-        start(rs_copy(way, k, h))
-
-    rs_step(0, 0, 0)
-    rs_step(1, 0, 1)
-    rs_step(0, 1, 1)
-    rs_step(1, 1, 0)
 
     pg_all = pg_v[...]
     pg_v[...] = pg_all.astype(BF).astype(F32)
@@ -276,32 +295,34 @@
         items[:, group_rows(g), :] = jnp.where(lane_g < 64, grads[0], grads[1]).astype(BF).reshape(F, 16, 128)
         return carry
 
-    lax.fori_loop(0, B // 16, emb_step, 0)
-
-    rs_step(0, 1, 0)
-    rs_step(1, 1, 1)
-
-    def x_copy(i):
-        return rcopy(x_s, x_r.at[me_d], x_ss.at[i], x_rs.at[me_d], dp=(me_d + i) % DP)
+    lax.fori_loop(0, 4, emb_step, 0, unroll=2)
+    for t, j in enumerate((opp_o, left_o, right_o)):
+        twin_copy(5 + t, j).wait_recv()
+    rs_round(True, 0)
+    rs_round(False, 2)
+    lax.fori_loop(4, 8, emb_step, 0, unroll=2)
 
     x_tile = dot(hotx_v[...], items[...].reshape(B * F, 128))
     row_x = lax.broadcasted_iota(jnp.int32, (XROWS, 128), 0)
     ids_x = jnp.concatenate([ids_x, jnp.zeros((ids_x.shape[0], 128 - XROWS), F32)], axis=1)
     x_tile = jnp.where(row_x == 66, ids_x[2:3], jnp.where(row_x == 67, ids_x[3:4], x_tile))
-    x_s[...] = x_tile.astype(BF)
-    x_r[me_d] = x_tile.astype(BF)
-
-    def x_start(i, carry):
+    x_v[core, yh, z, :XROWS] = x_tile.astype(BF)
+    x_own = x_v.at[core, yh, z, pl.ds(0, XROWS)]
+
+    def x_copy(i):
+        return rcopy(x_own, x_own, x_ss.at[i], x_rs.at[z], dp=(me_d + 4 * i) % DP)
+
+    for i in (4, 3, 5, 2, 6, 1, 7):
         x_copy(i).start()
-        return carry
-
-    lax.fori_loop(1, DP, x_start, 0)
 
     def a_copy(o):
         return rcopy(send_v.at[o], recv_v.at[me_d], a_ss.at[o], a_rs.at[me_d], dp=o)
 
+    def turn(i):
+        return 4 + (2 * (i % 2) - 1) * ((i + 1) // 2)
+
     def a_step(i, carry):
-        k = (z + 4 + i) % 8
+        k = (z + turn(i)) % 8
         tile = dot(hot_v[k], items[...].reshape(B * F, 128))
         row = lax.broadcasted_iota(jnp.int32, (64, 128), 0)
         for q in range(4):
@@ -318,20 +339,18 @@
                 a_copy(o).start()
         return carry
 
+    rs_round(True, 1)
+    rs_round(False, 3)
     lax.fori_loop(0, 4, a_step, 0)
-    for way in range(2):
-        rs_step(way, 2, 0)
-        rs_step(way, 2, 1)
+    rs_round(True, 2)
     lax.fori_loop(4, 8, a_step, 0)
-    for way in range(2):
-        rs_step(way, 3, 0)
-        rs_step(way, 3, 1)
+    rs_round(True, 3)
 
     tg_ref[...] = jnp.zeros_like(tg_ref)
     row_id = lax.broadcasted_iota(jnp.int32, (ROWS_DEV, 128), 0).astype(F32)
 
     def a_add(i, carry):
-        k = (z + 8 - i) % 8
+        k = (z + 8 - turn(i)) % 8
         low = lax.broadcasted_iota(jnp.int32, (8, 128), 1) < 64
         dead = lax.broadcasted_iota(jnp.int32, (8, 128), 1) % 64 >= KEEP
         for q in range(4):
@@ -341,8 +360,8 @@
         ids = []
         for q in range(4):
             got = jnp.broadcast_to(recv_v[k * 4 + q, KEEP:KEEP + 1, :].astype(F32), (8, 128))
-            turn = pltpu.roll(got, 64, 1)
-            ids.append(got + 256 * turn if q % 2 == 0 else turn + 256 * got)
+            swapped = pltpu.roll(got, 64, 1)
+            ids.append(got + 256 * swapped if q % 2 == 0 else swapped + 256 * got)
         hots = []
         for m in range(2):
             both = jnp.where(dead, -1.0, jnp.where(low, ids[2 * m], ids[2 * m + 1]))[0:1]
@@ -351,7 +370,13 @@
         tg_ref[...] += dot(jnp.concatenate(hots, axis=1), values)
         return carry
 
-    lax.fori_loop(0, 8, a_add, 0)
+    for i in range(1, 8):
+        block = x_v.at[core, yh, (z + 8 - i) % 8, pl.ds(0, XROWS)]
+        rcopy(block, block, x_ss.at[0], x_rs.at[(z + 8 - i) % 8], dp=twin).wait_recv()
+    x_half = x_v.at[core, yh, :, pl.ds(0, XROWS)]
+    start(rcopy(x_half, x_half, x_ss.at[8], x_rs.at[8], dp=y_part))
+
+    lax.fori_loop(0, 4, a_add, 0)
 
     for way in range(2):
         for h in range(2):
@@ -362,40 +387,57 @@
 
     y_s[...] = whole(1 - yh).astype(BF)
     y_copy = rcopy(y_s, y_r, y_ss, y_rs, dp=y_part)
-    y_copy.start()
-
+    start(y_copy)
+
+    other = x_v.at[core, 1 - yh, :, pl.ds(0, XROWS)]
+    rcopy(other, other, x_ss.at[8], x_rs.at[8], dp=y_part).wait_recv()
+    x_all = x_v.at[core, :, :, pl.ds(0, XROWS)]
+    start(rcopy(x_all, x_all, x_ss.at[9], x_rs.at[9], dp=twin))
+
+    lax.fori_loop(4, 8, a_add, 0)
+    last = whole(yh)
+    y_copy.wait_recv()
+    wg_ref[...] = (last + y_r[...].astype(F32)).astype(BF)
+
+    x_twin = x_v.at[1 - core, :, :, pl.ds(0, XROWS)]
+    rcopy(x_twin, x_twin, x_ss.at[9], x_rs.at[9], dp=twin).wait_recv()
     base = (me_d * ROWS_DEV).astype(F32)
+    live = lax.broadcasted_iota(jnp.int32, (1, 128), 1) < 66
 
     def x_add(i, carry):
-        src = (me_d + i) % DP
-
-        @pl.when(src != me_d)
-        def _():
-            rcopy(x_s, x_r.at[src], x_ss.at[0], x_rs.at[src], dp=twin).wait_recv()
-
-        low = x_r[src, 66:67, :].astype(F32)
-        high = x_r[src, 67:68, :].astype(F32)
-        ids = low + 128 * high - base
-        ids = jnp.where(lax.broadcasted_iota(jnp.int32, (1, 128), 1) < 66, ids, -1.0)
-        hot = jnp.where(row_id == ids, 1.0, 0.0).astype(BF)
-        tg_ref[...] += dot(hot[:, :XROWS], x_r[src])
-        return carry
-
-    lax.fori_loop(0, DP, x_add, 0)
-
-    last = whole(yh)
-    y_copy.wait()
-    wg_ref[...] = (last + y_r[...].astype(F32)).astype(BF)
+        hots = []
+        for q in range(4):
+            low = x_v[i // 4, (i // 2) % 2, (i % 2) * 4 + q, 66:67, :].astype(F32)
+            high = x_v[i // 4, (i // 2) % 2, (i % 2) * 4 + q, 67:68, :].astype(F32)
+            ids = jnp.where(live, low + 128 * high - base, -1.0)
+            hots.append(jnp.where(row_id == ids, 1.0, 0.0).astype(BF))
+        block = pl.ds(pl.multiple_of((i % 2) * 4, 4), 4)
+        values = x_v[i // 4, (i // 2) % 2, block].reshape(512, 128)
+        tg_ref[...] += dot(jnp.concatenate(hots, axis=1), values)
+        return carry
+
+    lax.fori_loop(0, 8, x_add, 0)
 
     for copy in sent:
         copy.wait_send()
+    for i in range(1, 8):
+        x_copy(i).wait_send()
+    for way in range(2):
+        for k in range(4):
+            for h in range(2):
+                if k > 0 or h == way:
+                    rs_copy(way, k, h).wait_send()
 
     def drain(i, carry):
-        x_copy(i).wait_send()
         a_copy((me_d + i) % DP).wait_send()
         return carry
 
     lax.fori_loop(1, DP, drain, 0)
+
+
+def hand_over(wg_in, tg_in, wg_out, tg_out):
+    wg_out[...] = wg_in[...]
+    tg_out[...] = tg_in[...]
 
 
 def on_device(embeddings, cotangent, first_weight, feature_rows):
@@ -403,12 +445,17 @@
     hbm = pl.BlockSpec(memory_space=pl.ANY)
     dma = pltpu.SemaphoreType.DMA
     consts = [jnp.asarray(a) for a in constants()]
-    return pl.pallas_call(
+    shapes = (jax.ShapeDtypeStruct((2 * PAIRS, 256), BF), jax.ShapeDtypeStruct((ROWS_DEV, 128), F32))
+    results = pl.pallas_call(
         kernel,
-        out_shape=(jax.ShapeDtypeStruct((2 * PAIRS, 256), BF), jax.ShapeDtypeStruct((ROWS_DEV, 128), F32)),
-        in_specs=[vmem, hbm, hbm, vmem, vmem, vmem, vmem],
+        out_shape=shapes,
+        in_specs=[hbm, hbm, hbm, vmem, hbm, hbm, hbm],
         out_specs=(vmem, vmem),
         scratch_shapes=[
+            pltpu.VMEM((2, B, 1024), BF),
+            pltpu.VMEM((256, 256), BF),
+            pltpu.VMEM((256, 128), BF),
+            pltpu.VMEM((256, 256), BF),
             pltpu.VMEM((8, 2, 2, B, 256), BF),
             pltpu.VMEM((8, 2, B, 256), BF),
             pltpu.VMEM((2 * PAIRS, 8192), BF),
@@ -417,7 +464,6 @@
             pltpu.VMEM((B, 256), F32),
             pltpu.VMEM((2 * PAIRS, 256), BF),
             pltpu.VMEM((B, 256), F32),
-            pltpu.VMEM((B, 128), F32),
             pltpu.VMEM((F, 128), jnp.int32),
             pltpu.VMEM((16, B * F), F32),
             pltpu.VMEM((8, 8, 128), F32),
@@ -429,15 +475,20 @@
             pltpu.VMEM((2 * PAIRS, 256), BF),
             pltpu.VMEM((DP, 64, 128), BF),
             pltpu.VMEM((DP, 64, 128), BF),
-            pltpu.VMEM((XROWS, 128), BF),
-            pltpu.VMEM((DP, XROWS, 128), BF),
-            dma((5,)), dma((9,)), dma((9,)), dma((8,)), dma((8,)), dma, dma,
+            pltpu.VMEM((2, 2, 8, 128, 128), BF),
+            dma((9,)), dma((11,)), dma((11,)), dma((8,)), dma((8,)), dma, dma,
             dma((2, 4, 2)), dma((2, 4, 2)), dma, dma,
-            dma((DP,)), dma((DP,)), dma((DP,)), dma((DP,)),
+            dma((DP,)), dma((DP,)), dma((10,)), dma((10,)),
         ],
         compiler_params=pltpu.CompilerParams(
             collective_id=0, has_side_effects=True, vmem_limit_bytes=56 * 1024 * 1024),
-    )(embeddings, cotangent, first_weight, feature_rows, *consts)
+    )(embeddings, cotangent, first_weight, feature_rows.T, *consts)
+    return pl.pallas_call(
+        hand_over,
+        out_shape=shapes,
+        in_specs=[vmem, vmem],
+        out_specs=(vmem, vmem),
+    )(*results)
 
 
 def solution(mesh):

time: 96.4 us -> 78.7 us (0.82)
  Pallas kernels: 91 us -> 77.1 us
  local copies, waits for them, and re-layouts: 4.65 us -> 0 us
    pallas_call x1 -> x2, Pallas kernels: 91 us -> 77.1 us  [the longest x1 75.3 us: on_device(): pl.pallas_call(kernel, out_shape=shapes, in_specs=[hbm, hbm, hbm, vmem, h...]
    unnamed x3 -> x0, local copies, waits for them, and re-layouts: 4.65 us -> none
where the time goes in v2:
time: 78.7 us; the launch traced here: 77.7 us
  Pallas kernels  77.1 us (98%)
    pallas_call x1, Pallas kernels, on_device(): pl.pallas_call(kernel, out_shape=shapes, in_specs=[hbm, hbm, hbm, vmem, h...  75.3 us
    pallas_call x1, Pallas kernels, on_device(): pl.pallas_call(hand_over, out_shape=shapes, in_specs=[vmem, vmem], out_sp...  1.77 us

profile of v2, /device:TPU:1, one launch (start us, length us, event | category | flops | bytes accessed | tf_op | source)
XLA Modules:
  0.0 77.7 jit_solution(1381250810520905990)
XLA Ops:
  0.6 75.3 %shard_map.86 = (bf16[240,256]{1,0:T(8,128)(2,1)}, f32[512,128]{1,0:T(8,128)}) custom-call(bf16[2,128,1024]{2,1,0:T(8,128)(2,1)} %emb_hbm.1, bf16[128,1024]{1,0:T(8,128)(2,1)} %cot_ref.1, bf16[240,8192]{1,0:T(8,128)(2,1)} %w_ref.1, s32[16,128]{1,0:T(8,128)} %bitcast.1, bf16[256,256]{1,0:T(8,128)(2,1)} %constant.6.clone.spread_hbm, ...), custom_call_target="tpu_custom_call" | custom-call | tf_op jit(solution)/shard_map/pallas_call | solution.py:449
  76.0 1.8 %shard_map.87 = (bf16[240,256]{1,0:T(8,128)(2,1)}, f32[512,128]{1,0:T(8,128)}) custom-call(bf16[240,256]{1,0:T(8,128)(2,1)} %get-tuple-element.4.wg_in, f32[512,128]{1,0:T(8,128)} %get-tuple-element.5.tg_in), custom_call_target="tpu_custom_call" | custom-call | tf_op jit(solution)/shard_map/pallas_call | solution.py:486

commit v3 on v2

--- a/solution.py
+++ b/solution.py
@@ -45,9 +45,9 @@
 
 def kernel(emb_hbm, cot_ref, w_ref, rows_ref, spread_hbm, pick_hbm, mask_hbm, wg_ref, tg_ref,
            emb_ref, spread_ref, pick_ref, mask_ref,
-           cot_v, sib_v, w_v, ei, items, pairs_v, pt_v, pg_v, pos_v, vals_v, meta_v,
-           hot_v, hotx_v, rs_s, rs_r, y_s, y_r, send_v, recv_v, x_v,
-           loc_sem, ag_ss, ag_rs, sib_ss, sib_rs, pt_ss, pt_rs, rs_ss, rs_rs, y_ss, y_rs,
+           cot_v, cz_v, w_v, ei, items, pairs_v, pt_v, pg_v, pos_v, vals_v, meta_v,
+           hot_v, hotx_v, wp_f, wp_s, wp_r, ws_s, ws_r, send_v, recv_v, x_v,
+           loc_sem, ag_ss, ag_rs, cz_ss, cz_rs, pt_ss, pt_rs, wp_ss, wp_rs, ws_ss, ws_rs,
            a_ss, a_rs, x_ss, x_rs):
     me_s = lax.axis_index("set")
     me_d = lax.axis_index("dp")
@@ -62,7 +62,7 @@
     z, yh, core = me_d // 4, (me_d // 2) % 2, me_d % 2
     twin = me_d + 1 - 2 * core
     y_part = me_d + 2 - 4 * yh
-    z_up, z_down = (me_d + 4) % DP, (me_d + 28) % DP
+    unit = me_d % 4
 
     def rcopy(src, dst, ss, rs, **where):
         return pltpu.make_async_remote_copy(
@@ -75,7 +75,9 @@
                 cot_ref.at[:, pl.ds((h * 2 + cc) * 256, 256)], cot_v.at[me_s, cc, h], loc_sem.at[h * 2 + cc]))
     inputs = ((emb_hbm, emb_ref), (pick_hbm, pick_ref), (mask_hbm, mask_ref), (spread_hbm, spread_ref), (w_ref, w_v))
     in_copies = [pltpu.make_async_copy(a, b, loc_sem.at[4 + i]) for i, (a, b) in enumerate(inputs)]
-    for copy in own_copies + in_copies:
+    own_cz = pltpu.make_async_copy(cot_ref.at[:, pl.ds(pl.multiple_of(z * 128, 128), 128)],
+                                   cz_v.at[me_s, z // 4, z % 4], loc_sem.at[9])
+    for copy in own_copies + [own_cz] + in_copies:
         copy.start()
 
     barrier = pltpu.get_barrier_semaphore()
@@ -97,25 +99,54 @@
         copy.start()
         sent.append(copy)
 
-    def ag(k, src, peer):
-        start(rcopy(src, src, ag_ss.at[k], ag_rs.at[k], set=peer))
-
-    def ag_wait(k, block):
-        rcopy(block, block, ag_ss.at[k], ag_rs.at[k], set=right).wait_recv()
-
-    ag(0, cot_v.at[me_s, 0], right)
-    ag(2, cot_v.at[me_s, 1], left)
-    ag(4, cot_v.at[me_s], over)
-    ag(1, cot_v.at[me_s, 1], right)
-    ag(3, cot_v.at[me_s, 0], left)
-
-    def twin_copy(t, j):
-        return rcopy(cot_v.at[j, 1 - core], sib_v.at[j], sib_ss.at[t], sib_rs.at[t], dp=twin)
-
-    def to_twin(t, j):
-        start(twin_copy(t, j))
-
-    to_twin(0, me_s)
+    def ag(g, k, src, peer):
+        start(rcopy(src, src, ag_ss.at[g, k], ag_rs.at[g, k], set=peer))
+
+    def ag_wait(g, k, block):
+        rcopy(block, block, ag_ss.at[g, k], ag_rs.at[g, k], set=right).wait_recv()
+
+    def ag_own(g, buf):
+        ag(g, 0, buf.at[me_s, 0], right)
+        ag(g, 2, buf.at[me_s, 1], left)
+        ag(g, 4, buf.at[me_s], over)
+        ag(g, 1, buf.at[me_s, 1], right)
+        ag(g, 3, buf.at[me_s, 0], left)
+
+    def ag_halves(g, buf):
+        ag_wait(g, 0, buf.at[left, 0])
+        ag(g, 5, buf.at[left, 0], right)
+        ag_wait(g, 2, buf.at[right, 1])
+        ag(g, 6, buf.at[right, 1], left)
+
+    def ag_over(g, buf):
+        ag_wait(g, 4, buf.at[over])
+        ag(g, 7, buf.at[over], right)
+        ag(g, 8, buf.at[over], left)
+
+    def ag_near(g, buf):
+        ag_wait(g, 1, buf.at[left, 1])
+        ag_wait(g, 3, buf.at[right, 0])
+
+    def ag_opp(g, buf):
+        ag_wait(g, 5, buf.at[opp, 0])
+        ag(g, 9, buf.at[opp, 0], over)
+        ag_wait(g, 6, buf.at[opp, 1])
+        ag(g, 10, buf.at[opp, 1], over)
+
+    def ag_opp_o(g, buf):
+        ag_wait(g, 9, buf.at[opp_o, 0])
+        ag_wait(g, 10, buf.at[opp_o, 1])
+
+    ag_own(0, cot_v)
+
+    def cz_copy(i):
+        q = (z + i) % 8
+        return rcopy(cot_ref.at[:, pl.ds(pl.multiple_of(q * 128, 128), 128)], cz_v.at[me_s, z // 4, z % 4],
+                     cz_ss.at[i], cz_rs.at[z], dp=(me_d + 4 * i) % DP)
+
+    far_first = (4, 3, 5, 2, 6, 1, 7)
+    for i in far_first:
+        start(cz_copy(i))
 
     for copy in in_copies[:4]:
         copy.wait()
@@ -146,25 +177,20 @@
 
     lax.fori_loop(0, 4, pair_step, 0)
 
-    ag_wait(0, cot_v.at[left, 0])
-    ag(5, cot_v.at[left, 0], right)
-    ag_wait(2, cot_v.at[right, 1])
-    ag(6, cot_v.at[right, 1], left)
-
+    ag_halves(0, cot_v)
     lax.fori_loop(4, 8, pair_step, 0)
     turned = pairs_v[...].T
-    pt_v[:, :B] = jnp.concatenate([turned[:PAIRS], turned[128:128 + PAIRS]], axis=0).astype(BF)
-    pt_copy = rcopy(pt_v.at[:, pl.ds(0, B)], pt_v.at[:, pl.ds(B, B)], pt_ss, pt_rs, dp=twin)
-    start(pt_copy)
-
-    ag_wait(4, cot_v.at[over])
-    ag(7, cot_v.at[over], right)
-    ag(8, cot_v.at[over], left)
-    to_twin(1, over)
-    ag_wait(1, cot_v.at[left, 1])
-    ag_wait(3, cot_v.at[right, 0])
-    to_twin(2, left)
-    to_twin(3, right)
+    own_pairs = pl.ds(pl.multiple_of(z * B, B), B)
+    pt_v[:, own_pairs] = jnp.concatenate([turned[:PAIRS], turned[128:128 + PAIRS]], axis=0).astype(BF)
+
+    def pt_copy(i):
+        return rcopy(pt_v.at[:, own_pairs], pt_v.at[:, own_pairs], pt_ss.at[i], pt_rs.at[z], dp=(me_d + 4 * i) % DP)
+
+    for i in far_first:
+        start(pt_copy(i))
+
+    ag_over(0, cot_v)
+    ag_near(0, cot_v)
 
     in_copies[4].wait()
     pg_v[...] = jnp.zeros_like(pg_v)
@@ -178,42 +204,49 @@
                 total = term if total is None else total + term
         pg_v[:, :2 * PAIRS] += total
 
-    def part(j, h):
-        return dot(pt_v[...], jnp.concatenate([cot_v[j, core, h], sib_v[j, h]], axis=0))
-
-    def rs_copy(way, k, h):
-        return rcopy(rs_s.at[way, k, h], rs_r.at[way, k, h], rs_ss.at[way, k, h], rs_rs.at[way, k, h],
-                     dp=z_up if way else z_down)
-
-    def rs_step(late, way, k, h):
-        j = (z + 12 - k) % 8 if way else (z + 4 + k) % 8
-        is_late = (j == left_o) | (j == right_o) | (j == opp_o)
-
-        @pl.when(is_late if late else jnp.logical_not(is_late))
+    def wp_copy(j, i):
+        to = (unit + i) % 4
+        return rcopy(wp_s.at[j, pl.ds(pl.multiple_of(to * 64, 64), 64)], wp_r.at[j, unit],
+                     wp_ss.at[j, i], wp_rs.at[j, unit], dp=z * 4 + to)
+
+    def wp_make(j):
+        value = dot(pt_v[...], cz_v[j].reshape(8 * B, 128))
+        value = jnp.concatenate([value, jnp.zeros((16, 128), F32)], axis=0)
+        wp_f[j] = value
+        wp_s[j] = value.astype(BF)
+        for i in (2, 3, 1):
+            start(wp_copy(j, i))
+
+    def ws_copy(j):
+        return rcopy(ws_s.at[j], ws_r.at[z % 2, unit], ws_ss.at[j], ws_rs.at[z % 2, unit], dp=j * 4 + z // 2)
+
+    def ws_make(j):
+        total = wp_f[j, pl.ds(pl.multiple_of(unit * 64, 64), 64)]
+        for i in (1, 3, 2):
+            source = (unit + i) % 4
+            rcopy(wp_s.at[j, pl.ds(0, 64)], wp_r.at[j, source], wp_ss.at[j, i], wp_rs.at[j, source], dp=twin).wait_recv()
+            total = total + wp_r[j, source].astype(F32)
+        block = total.astype(BF)
+        ws_s[j] = block
+        here = j * 4 + z // 2 == me_d
+
+        @pl.when(here)
         def _():
-            value = part(j, h)
-            if k >= 2 or (k == 1 and h == way):
-                rs_copy(way, k - 1, h).wait_recv()
-                value = value + rs_r[way, k - 1, h].astype(F32)
-            rs_s[way, k, h] = value.astype(BF)
-            rs_copy(way, k, h).start()
-
-    def rs_round(late, n):
-        for way in range(2):
-            if n < 4:
-                rs_step(late, way, n, way)
-        for way in range(2):
-            if n < 3:
-                rs_step(late, way, n + 1, 1 - way)
+            ws_r[z % 2, unit] = block
+
+        @pl.when(jnp.logical_not(here))
+        def _():
+            ws_copy(j).start()
 
     for j in (me_s, over, left, right):
         pg_add(j)
 
-    ag_wait(5, cot_v.at[opp, 0])
-    ag(9, cot_v.at[opp, 0], over)
-    ag_wait(6, cot_v.at[opp, 1])
-    ag(10, cot_v.at[opp, 1], over)
-    to_twin(4, opp)
+    ag_opp(0, cot_v)
+    own_cz.wait()
+    for i in range(1, 8):
+        block = cz_v.at[me_s, ((z + i) % 8) // 4, (z + i) % 4]
+        rcopy(block, block, cz_ss.at[i], cz_rs.at[(z + i) % 8], dp=twin).wait_recv()
+    ag_own(1, cz_v)
 
     rows_t = rows_ref[...].astype(F32)
     owner = jnp.floor(rows_t * (1.0 / ROWS_DEV))
@@ -254,10 +287,6 @@
             meta_v[k, q:q + 1, :] = row
         return carry
 
-    pt_copy.wait_recv()
-    for t, j in enumerate((me_s, over, left, right, opp)):
-        twin_copy(t, j).wait_recv()
-    rs_round(False, 0)
     pg_add(opp)
     lax.fori_loop(0, 8, hot_step, 0)
     slot_x = lax.broadcasted_iota(jnp.int32, (XROWS, 128), 0) + DP * 64
@@ -265,16 +294,11 @@
         hotx_v[:, f * 128:(f + 1) * 128] = jnp.where(slot_x == pos_v[f:f + 1, :], 1.0, 0.0).astype(BF)
     ids_x = dot_nt(vals_v[...].astype(BF), hotx_v[...])
     x_v[:, :, :, XROWS:] = jnp.zeros((2, 2, 8, 128 - XROWS, 128), BF)
-    rs_round(False, 1)
-
-    ag_wait(9, cot_v.at[opp_o, 0])
-    ag_wait(10, cot_v.at[opp_o, 1])
-    to_twin(5, opp_o)
+
+    ag_opp_o(0, cot_v)
     pg_add(opp_o)
-    ag_wait(7, cot_v.at[left_o])
-    to_twin(6, left_o)
-    ag_wait(8, cot_v.at[right_o])
-    to_twin(7, right_o)
+    ag_wait(0, 7, cot_v.at[left_o])
+    ag_wait(0, 8, cot_v.at[right_o])
     pg_add(left_o)
     pg_add(right_o)
 
@@ -295,12 +319,10 @@
         items[:, group_rows(g), :] = jnp.where(lane_g < 64, grads[0], grads[1]).astype(BF).reshape(F, 16, 128)
         return carry
 
-    lax.fori_loop(0, 4, emb_step, 0, unroll=2)
-    for t, j in enumerate((opp_o, left_o, right_o)):
-        twin_copy(5 + t, j).wait_recv()
-    rs_round(True, 0)
-    rs_round(False, 2)
-    lax.fori_loop(4, 8, emb_step, 0, unroll=2)
+    lax.fori_loop(0, 2, emb_step, 0, unroll=2)
+    ag_halves(1, cz_v)
+    lax.fori_loop(2, 8, emb_step, 0, unroll=3)
+    ag_over(1, cz_v)
 
     x_tile = dot(hotx_v[...], items[...].reshape(B * F, 128))
     row_x = lax.broadcasted_iota(jnp.int32, (XROWS, 128), 0)
@@ -312,8 +334,8 @@
     def x_copy(i):
         return rcopy(x_own, x_own, x_ss.at[i], x_rs.at[z], dp=(me_d + 4 * i) % DP)
 
-    for i in (4, 3, 5, 2, 6, 1, 7):
-        x_copy(i).start()
+    for i in far_first:
+        start(x_copy(i))
 
     def a_copy(o):
         return rcopy(send_v.at[o], recv_v.at[me_d], a_ss.at[o], a_rs.at[me_d], dp=o)
@@ -339,12 +361,17 @@
                 a_copy(o).start()
         return carry
 
-    rs_round(True, 1)
-    rs_round(False, 3)
     lax.fori_loop(0, 4, a_step, 0)
-    rs_round(True, 2)
+    ag_near(1, cz_v)
+    ag_opp(1, cz_v)
     lax.fori_loop(4, 8, a_step, 0)
-    rs_round(True, 3)
+
+    for i in range(1, 8):
+        block = pt_v.at[:, pl.ds(pl.multiple_of((z + i) % 8 * B, B), B)]
+        rcopy(block, block, pt_ss.at[i], pt_rs.at[(z + i) % 8], dp=twin).wait_recv()
+    early = (me_s, over, left, right, opp)
+    for j in early:
+        wp_make(j)
 
     tg_ref[...] = jnp.zeros_like(tg_ref)
     row_id = lax.broadcasted_iota(jnp.int32, (ROWS_DEV, 128), 0).astype(F32)
@@ -376,18 +403,17 @@
     x_half = x_v.at[core, yh, :, pl.ds(0, XROWS)]
     start(rcopy(x_half, x_half, x_ss.at[8], x_rs.at[8], dp=y_part))
 
+    ag_opp_o(1, cz_v)
+    wp_make(opp_o)
+    ag_wait(1, 7, cz_v.at[left_o])
+    wp_make(left_o)
+    ag_wait(1, 8, cz_v.at[right_o])
+    wp_make(right_o)
+    for j in early:
+        ws_make(j)
     lax.fori_loop(0, 4, a_add, 0)
-
-    for way in range(2):
-        for h in range(2):
-            rs_copy(way, 3, h).wait_recv()
-
-    def whole(h):
-        return part(z, h) + rs_r[0, 3, h].astype(F32) + rs_r[1, 3, h].astype(F32)
-
-    y_s[...] = whole(1 - yh).astype(BF)
-    y_copy = rcopy(y_s, y_r, y_ss, y_rs, dp=y_part)
-    start(y_copy)
+    for j in (opp_o, left_o, right_o):
+        ws_make(j)
 
     other = x_v.at[core, 1 - yh, :, pl.ds(0, XROWS)]
     rcopy(other, other, x_ss.at[8], x_rs.at[8], dp=y_part).wait_recv()
@@ -395,38 +421,45 @@
     start(rcopy(x_all, x_all, x_ss.at[9], x_rs.at[9], dp=twin))
 
     lax.fori_loop(4, 8, a_add, 0)
-    last = whole(yh)
-    y_copy.wait_recv()
-    wg_ref[...] = (last + y_r[...].astype(F32)).astype(BF)
-
+
+    base = (me_d * ROWS_DEV).astype(F32)
+    live = lax.broadcasted_iota(jnp.int32, (1, 128), 1) < 66
+
+    def x_add(cc):
+        def body(i, carry):
+            half, first = i // 2, (i % 2) * 4
+            hots = []
+            for q in range(4):
+                low = x_v[cc, half, first + q, 66:67, :].astype(F32)
+                high = x_v[cc, half, first + q, 67:68, :].astype(F32)
+                ids = jnp.where(live, low + 128 * high - base, -1.0)
+                hots.append(jnp.where(row_id == ids, 1.0, 0.0).astype(BF))
+            values = x_v[cc, half, pl.ds(pl.multiple_of(first, 4), 4)].reshape(512, 128)
+            tg_ref[...] += dot(jnp.concatenate(hots, axis=1), values)
+            return carry
+
+        lax.fori_loop(0, 4, body, 0)
+
+    x_add(core)
     x_twin = x_v.at[1 - core, :, :, pl.ds(0, XROWS)]
     rcopy(x_twin, x_twin, x_ss.at[9], x_rs.at[9], dp=twin).wait_recv()
-    base = (me_d * ROWS_DEV).astype(F32)
-    live = lax.broadcasted_iota(jnp.int32, (1, 128), 1) < 66
-
-    def x_add(i, carry):
-        hots = []
-        for q in range(4):
-            low = x_v[i // 4, (i // 2) % 2, (i % 2) * 4 + q, 66:67, :].astype(F32)
-            high = x_v[i // 4, (i // 2) % 2, (i % 2) * 4 + q, 67:68, :].astype(F32)
-            ids = jnp.where(live, low + 128 * high - base, -1.0)
-            hots.append(jnp.where(row_id == ids, 1.0, 0.0).astype(BF))
-        block = pl.ds(pl.multiple_of((i % 2) * 4, 4), 4)
-        values = x_v[i // 4, (i // 2) % 2, block].reshape(512, 128)
-        tg_ref[...] += dot(jnp.concatenate(hots, axis=1), values)
-        return carry
-
-    lax.fori_loop(0, 8, x_add, 0)
+    x_add(1 - core)
+
+    for half in range(2):
+        for source in range(4):
+            @pl.when((unit * 2 + half) * 4 + source != me_d)
+            def _():
+                rcopy(ws_s.at[0], ws_r.at[half, source], ws_ss.at[0], ws_rs.at[half, source], dp=twin).wait_recv()
+
+            rows = min(64, 2 * PAIRS - source * 64)
+            wg_ref[source * 64:source * 64 + rows, half * 128:(half + 1) * 128] = ws_r[half, source, :rows]
 
     for copy in sent:
         copy.wait_send()
-    for i in range(1, 8):
-        x_copy(i).wait_send()
-    for way in range(2):
-        for k in range(4):
-            for h in range(2):
-                if k > 0 or h == way:
-                    rs_copy(way, k, h).wait_send()
+    for j in range(8):
+        @pl.when(j * 4 + z // 2 != me_d)
+        def _():
+            ws_copy(j).wait_send()
 
     def drain(i, carry):
         a_copy((me_d + i) % DP).wait_send()
@@ -457,27 +490,28 @@
             pltpu.VMEM((256, 128), BF),
             pltpu.VMEM((256, 256), BF),
             pltpu.VMEM((8, 2, 2, B, 256), BF),
-            pltpu.VMEM((8, 2, B, 256), BF),
+            pltpu.VMEM((8, 2, 4, B, 128), BF),
             pltpu.VMEM((2 * PAIRS, 8192), BF),
             pltpu.VMEM((F, B, 128), BF),
             pltpu.VMEM((F, B, 128), BF),
             pltpu.VMEM((B, 256), F32),
-            pltpu.VMEM((2 * PAIRS, 256), BF),
+            pltpu.VMEM((2 * PAIRS, 8 * B), BF),
             pltpu.VMEM((B, 256), F32),
             pltpu.VMEM((F, 128), jnp.int32),
             pltpu.VMEM((16, B * F), F32),
             pltpu.VMEM((8, 8, 128), F32),
             pltpu.VMEM((8, 256, B * F), BF),
             pltpu.VMEM((XROWS, B * F), BF),
-            pltpu.VMEM((2, 4, 2, 2 * PAIRS, 256), BF),
-            pltpu.VMEM((2, 4, 2, 2 * PAIRS, 256), BF),
-            pltpu.VMEM((2 * PAIRS, 256), BF),
-            pltpu.VMEM((2 * PAIRS, 256), BF),
+            pltpu.VMEM((8, 256, 128), F32),
+            pltpu.VMEM((8, 256, 128), BF),
+            pltpu.VMEM((8, 4, 64, 128), BF),
+            pltpu.VMEM((8, 64, 128), BF),
+            pltpu.VMEM((2, 4, 64, 128), BF),
             pltpu.VMEM((DP, 64, 128), BF),
             pltpu.VMEM((DP, 64, 128), BF),
             pltpu.VMEM((2, 2, 8, 128, 128), BF),
-            dma((9,)), dma((11,)), dma((11,)), dma((8,)), dma((8,)), dma, dma,
-            dma((2, 4, 2)), dma((2, 4, 2)), dma, dma,
+            dma((10,)), dma((2, 11)), dma((2, 11)), dma((8,)), dma((8,)), dma((8,)), dma((8,)),
+            dma((8, 4)), dma((8, 4)), dma((8,)), dma((2, 4)),
             dma((DP,)), dma((DP,)), dma((10,)), dma((10,)),
         ],
         compiler_params=pltpu.CompilerParams(

time: 78.7 us -> 71.1 us (0.903); the launches traced: 77.7 us -> 71 us
  Pallas kernels: 77.1 us -> 70.3 us
    pallas_call x1, Pallas kernels: 75.3 us -> 68.6 us  [on_device(): pl.pallas_call(kernel, out_shape=shapes, in_specs=[hbm, hbm, hbm, vmem, h...]
where the time goes in v3:
time: 71.1 us; the launch traced here: 71 us
  Pallas kernels  70.3 us (99%)
    pallas_call x1, Pallas kernels, on_device(): pl.pallas_call(kernel, out_shape=shapes, in_specs=[hbm, hbm, hbm, vmem, h...  68.6 us
    pallas_call x1, Pallas kernels, on_device(): pl.pallas_call(hand_over, out_shape=shapes, in_specs=[vmem, vmem], out_sp...  1.77 us

profile of v3, /device:TPU:1, one launch (start us, length us, event | category | flops | bytes accessed | tf_op | source)
XLA Modules:
  0.0 71.0 jit_solution(13721025707819179947)
XLA Ops:
  0.6 68.6 %shard_map.86 = (bf16[240,256]{1,0:T(8,128)(2,1)}, f32[512,128]{1,0:T(8,128)}) custom-call(bf16[2,128,1024]{2,1,0:T(8,128)(2,1)} %emb_hbm.1, bf16[128,1024]{1,0:T(8,128)(2,1)} %cot_ref.1, bf16[240,8192]{1,0:T(8,128)(2,1)} %w_ref.1, s32[16,128]{1,0:T(8,128)} %bitcast.1, bf16[256,256]{1,0:T(8,128)(2,1)} %constant.6.clone.spread_hbm, ...), custom_call_target="tpu_custom_call" | custom-call | tf_op jit(solution)/shard_map/pallas_call | solution.py:482
  69.2 1.8 %shard_map.87 = (bf16[240,256]{1,0:T(8,128)(2,1)}, f32[512,128]{1,0:T(8,128)}) custom-call(bf16[240,256]{1,0:T(8,128)(2,1)} %get-tuple-element.4.wg_in, f32[512,128]{1,0:T(8,128)} %get-tuple-element.5.tg_in), custom_call_target="tpu_custom_call" | custom-call | tf_op jit(solution)/shard_map/pallas_call | solution.py:520

commit v4 on v3

--- a/solution.py
+++ b/solution.py
@@ -46,8 +46,8 @@
 def kernel(emb_hbm, cot_ref, w_ref, rows_ref, spread_hbm, pick_hbm, mask_hbm, wg_ref, tg_ref,
            emb_ref, spread_ref, pick_ref, mask_ref,
            cot_v, cz_v, w_v, ei, items, pairs_v, pt_v, pg_v, pos_v, vals_v, meta_v,
-           hot_v, hotx_v, wp_f, wp_s, wp_r, ws_s, ws_r, send_v, recv_v, x_v,
-           loc_sem, ag_ss, ag_rs, cz_ss, cz_rs, pt_ss, pt_rs, wp_ss, wp_rs, ws_ss, ws_rs,
+           hot_v, hotx_v, wp_f, wp_s, wp_r, ws_s, ws_r, wl_s, wl_r, send_v, recv_v, x_v,
+           loc_sem, ag_ss, ag_rs, cz_ss, cz_rs, pt_ss, pt_rs, wp_ss, wp_rs, ws_ss, ws_rs, wl_ss, wl_rs,
            a_ss, a_rs, x_ss, x_rs):
     me_s = lax.axis_index("set")
     me_d = lax.axis_index("dp")
@@ -237,6 +237,25 @@
         @pl.when(jnp.logical_not(here))
         def _():
             ws_copy(j).start()
+
+    late = (opp_o, left_o, right_o)
+    late_here = (z == opp_o) | (z == left_o) | (z == right_o)
+
+    def wl_copy(t):
+        return rcopy(wl_s.at[t], wl_r.at[z % 2, unit], wl_ss.at[t], wl_rs.at[z % 2, unit], dp=late[t] * 4 + z // 2)
+
+    def wl_make(t):
+        block = dot(pt_v[...], cz_v[late[t]].reshape(8 * B, 128)).astype(BF)
+        wl_s[t] = block
+        here = late[t] * 4 + z // 2 == me_d
+
+        @pl.when(here)
+        def _():
+            wl_r[z % 2, unit] = block
+
+        @pl.when(jnp.logical_not(here))
+        def _():
+            wl_copy(t).start()
 
     for j in (me_s, over, left, right):
         pg_add(j)
@@ -323,6 +342,10 @@
     ag_halves(1, cz_v)
     lax.fori_loop(2, 8, emb_step, 0, unroll=3)
     ag_over(1, cz_v)
+    for i in range(1, 8):
+        block = pt_v.at[:, pl.ds(pl.multiple_of((z + i) % 8 * B, B), B)]
+        rcopy(block, block, pt_ss.at[i], pt_rs.at[(z + i) % 8], dp=twin).wait_recv()
+    wp_make(me_s)
 
     x_tile = dot(hotx_v[...], items[...].reshape(B * F, 128))
     row_x = lax.broadcasted_iota(jnp.int32, (XROWS, 128), 0)
@@ -361,17 +384,18 @@
                 a_copy(o).start()
         return carry
 
-    lax.fori_loop(0, 4, a_step, 0)
+    lax.fori_loop(0, 2, a_step, 0)
     ag_near(1, cz_v)
+    for j in (over, left, right):
+        wp_make(j)
+    lax.fori_loop(2, 5, a_step, 0)
     ag_opp(1, cz_v)
-    lax.fori_loop(4, 8, a_step, 0)
-
-    for i in range(1, 8):
-        block = pt_v.at[:, pl.ds(pl.multiple_of((z + i) % 8 * B, B), B)]
-        rcopy(block, block, pt_ss.at[i], pt_rs.at[(z + i) % 8], dp=twin).wait_recv()
-    early = (me_s, over, left, right, opp)
-    for j in early:
-        wp_make(j)
+    wp_make(opp)
+    lax.fori_loop(5, 8, a_step, 0)
+
+    ws_make(me_s)
+    for j in (over, left, right):
+        ws_make(j)
 
     tg_ref[...] = jnp.zeros_like(tg_ref)
     row_id = lax.broadcasted_iota(jnp.int32, (ROWS_DEV, 128), 0).astype(F32)
@@ -397,23 +421,20 @@
         tg_ref[...] += dot(jnp.concatenate(hots, axis=1), values)
         return carry
 
+    ag_opp_o(1, cz_v)
+    wl_make(0)
+    ag_wait(1, 7, cz_v.at[left_o])
+    wl_make(1)
+    ag_wait(1, 8, cz_v.at[right_o])
+    wl_make(2)
     for i in range(1, 8):
         block = x_v.at[core, yh, (z + 8 - i) % 8, pl.ds(0, XROWS)]
         rcopy(block, block, x_ss.at[0], x_rs.at[(z + 8 - i) % 8], dp=twin).wait_recv()
     x_half = x_v.at[core, yh, :, pl.ds(0, XROWS)]
     start(rcopy(x_half, x_half, x_ss.at[8], x_rs.at[8], dp=y_part))
 
-    ag_opp_o(1, cz_v)
-    wp_make(opp_o)
-    ag_wait(1, 7, cz_v.at[left_o])
-    wp_make(left_o)
-    ag_wait(1, 8, cz_v.at[right_o])
-    wp_make(right_o)
-    for j in early:
-        ws_make(j)
+    ws_make(opp)
     lax.fori_loop(0, 4, a_add, 0)
-    for j in (opp_o, left_o, right_o):
-        ws_make(j)
 
     other = x_v.at[core, 1 - yh, :, pl.ds(0, XROWS)]
     rcopy(other, other, x_ss.at[8], x_rs.at[8], dp=y_part).wait_recv()
@@ -445,21 +466,39 @@
     rcopy(x_twin, x_twin, x_ss.at[9], x_rs.at[9], dp=twin).wait_recv()
     x_add(1 - core)
 
-    for half in range(2):
-        for source in range(4):
-            @pl.when((unit * 2 + half) * 4 + source != me_d)
-            def _():
-                rcopy(ws_s.at[0], ws_r.at[half, source], ws_ss.at[0], ws_rs.at[half, source], dp=twin).wait_recv()
-
-            rows = min(64, 2 * PAIRS - source * 64)
-            wg_ref[source * 64:source * 64 + rows, half * 128:(half + 1) * 128] = ws_r[half, source, :rows]
+    def from_line(half, source, block, arrived):
+        @pl.when((unit * 2 + half) * 4 + source != me_d)
+        def _():
+            rcopy(block, block, ws_ss.at[0], arrived, dp=twin).wait_recv()
+
+    @pl.when(late_here)
+    def _():
+        for half in range(2):
+            total = None
+            for source in range(4):
+                from_line(half, source, wl_r.at[half, source], wl_rs.at[half, source])
+                term = wl_r[half, source].astype(F32)
+                total = term if total is None else total + term
+            wg_ref[:, half * 128:(half + 1) * 128] = total.astype(BF)
+
+    @pl.when(jnp.logical_not(late_here))
+    def _():
+        for half in range(2):
+            for source in range(4):
+                from_line(half, source, ws_r.at[half, source], ws_rs.at[half, source])
+                rows = min(64, 2 * PAIRS - source * 64)
+                wg_ref[source * 64:source * 64 + rows, half * 128:(half + 1) * 128] = ws_r[half, source, :rows]
 
     for copy in sent:
         copy.wait_send()
-    for j in range(8):
+    for j in (me_s, over, left, right, opp):
         @pl.when(j * 4 + z // 2 != me_d)
         def _():
             ws_copy(j).wait_send()
+    for t in range(3):
+        @pl.when(late[t] * 4 + z // 2 != me_d)
+        def _():
+            wl_copy(t).wait_send()
 
     def drain(i, carry):
         a_copy((me_d + i) % DP).wait_send()
@@ -481,7 +520,7 @@
     shapes = (jax.ShapeDtypeStruct((2 * PAIRS, 256), BF), jax.ShapeDtypeStruct((ROWS_DEV, 128), F32))
     results = pl.pallas_call(
         kernel,
-        out_shape=shapes,
+        out_shape=(pltpu.VMEM((2 * PAIRS, 256), BF), pltpu.VMEM((ROWS_DEV, 128), F32)),
         in_specs=[hbm, hbm, hbm, vmem, hbm, hbm, hbm],
         out_specs=(vmem, vmem),
         scratch_shapes=[
@@ -507,11 +546,13 @@
             pltpu.VMEM((8, 4, 64, 128), BF),
             pltpu.VMEM((8, 64, 128), BF),
             pltpu.VMEM((2, 4, 64, 128), BF),
+            pltpu.VMEM((3, 2 * PAIRS, 128), BF),
+            pltpu.VMEM((2, 4, 2 * PAIRS, 128), BF),
             pltpu.VMEM((DP, 64, 128), BF),
             pltpu.VMEM((DP, 64, 128), BF),
             pltpu.VMEM((2, 2, 8, 128, 128), BF),
             dma((10,)), dma((2, 11)), dma((2, 11)), dma((8,)), dma((8,)), dma((8,)), dma((8,)),
-            dma((8, 4)), dma((8, 4)), dma((8,)), dma((2, 4)),
+            dma((8, 4)), dma((8, 4)), dma((8,)), dma((2, 4)), dma((3,)), dma((2, 4)),
             dma((DP,)), dma((DP,)), dma((10,)), dma((10,)),
         ],
         compiler_params=pltpu.CompilerParams(
@@ -522,7 +563,7 @@
         out_shape=shapes,
         in_specs=[vmem, vmem],
         out_specs=(vmem, vmem),
-    )(*results)
+    )(*[pltpu.with_memory_space_constraint(r, pltpu.VMEM) for r in results])
 
 
 def solution(mesh):

time: 71.1 us -> 67.5 us (0.949)
  the two profiles are of different devices: /device:TPU:1 before, /device:TPU:38 now
where the time goes in v4:
time: 67.5 us; the launch traced here: 67.3 us
  Pallas kernels  66.7 us (99%)
    pallas_call x1, Pallas kernels, on_device(): pl.pallas_call(kernel, out_shape=(pltpu.VMEM((2 * PAIRS, 256), BF), pltpu...  65.9 us

profile of v4, /device:TPU:38, one launch (start us, length us, event | category | flops | bytes accessed | tf_op | source)
XLA Modules:
  0.0 67.3 jit_solution(16151251532799443187)
XLA Ops:
  0.6 65.9 %shard_map.86 = (bf16[240,256]{1,0:T(8,128)(2,1)S(1)}, f32[512,128]{1,0:T(8,128)S(1)}) custom-call(bf16[2,128,1024]{2,1,0:T(8,128)(2,1)} %emb_hbm.1, bf16[128,1024]{1,0:T(8,128)(2,1)} %cot_ref.1, bf16[240,8192]{1,0:T(8,128)(2,1)} %w_ref.1, s32[16,128]{1,0:T(8,128)} %bitcast.1, bf16[256,256]{1,0:T(8,128)(2,1)} %constant.6.clone.spread_hbm, ...), custom_call_target="tpu_custom_call" | custom-call | tf_op jit(solution)/shard_map/pallas_call | solution.py:521
  66.6 0.8 %shard_map.87 = (bf16[240,256]{1,0:T(8,128)(2,1)}, f32[512,128]{1,0:T(8,128)}) custom-call(bf16[240,256]{1,0:T(8,128)(2,1)S(1)} %get-tuple-element.4.wg_in, f32[512,128]{1,0:T(8,128)S(1)} %get-tuple-element.5.tg_in), custom_call_target="tpu_custom_call" | custom-call | tf_op jit(solution)/shard_map/pallas_call | solution.py:561

commit v5 on v4

--- a/solution.py
+++ b/solution.py
@@ -99,6 +99,11 @@
         copy.start()
         sent.append(copy)
 
+    def settle():
+        for copy in sent:
+            copy.wait_send()
+        sent.clear()
+
     def ag(g, k, src, peer):
         start(rcopy(src, src, ag_ss.at[g, k], ag_rs.at[g, k], set=peer))
 
@@ -129,9 +134,11 @@
 
     def ag_opp(g, buf):
         ag_wait(g, 5, buf.at[opp, 0])
-        ag(g, 9, buf.at[opp, 0], over)
+        if g == 0:
+            ag(g, 9, buf.at[opp, 0], over)
         ag_wait(g, 6, buf.at[opp, 1])
-        ag(g, 10, buf.at[opp, 1], over)
+        if g == 0:
+            ag(g, 10, buf.at[opp, 1], over)
 
     def ag_opp_o(g, buf):
         ag_wait(g, 9, buf.at[opp_o, 0])
@@ -421,12 +428,15 @@
         tg_ref[...] += dot(jnp.concatenate(hots, axis=1), values)
         return carry
 
+    ag_wait(1, 7, cz_v.at[left_o])
+    ag(1, 9, cz_v.at[left_o, 0], right)
+    ag_wait(1, 8, cz_v.at[right_o])
+    ag(1, 10, cz_v.at[right_o, 1], left)
+    wl_make(1)
+    wl_make(2)
     ag_opp_o(1, cz_v)
     wl_make(0)
-    ag_wait(1, 7, cz_v.at[left_o])
-    wl_make(1)
-    ag_wait(1, 8, cz_v.at[right_o])
-    wl_make(2)
+    settle()
     for i in range(1, 8):
         block = x_v.at[core, yh, (z + 8 - i) % 8, pl.ds(0, XROWS)]
         rcopy(block, block, x_ss.at[0], x_rs.at[(z + 8 - i) % 8], dp=twin).wait_recv()
@@ -466,6 +476,12 @@
     rcopy(x_twin, x_twin, x_ss.at[9], x_rs.at[9], dp=twin).wait_recv()
     x_add(1 - core)
 
+    def drain(i, carry):
+        a_copy((me_d + i) % DP).wait_send()
+        return carry
+
+    lax.fori_loop(1, DP, drain, 0)
+
     def from_line(half, source, block, arrived):
         @pl.when((unit * 2 + half) * 4 + source != me_d)
         def _():
@@ -489,8 +505,7 @@
                 rows = min(64, 2 * PAIRS - source * 64)
                 wg_ref[source * 64:source * 64 + rows, half * 128:(half + 1) * 128] = ws_r[half, source, :rows]
 
-    for copy in sent:
-        copy.wait_send()
+    settle()
     for j in (me_s, over, left, right, opp):
         @pl.when(j * 4 + z // 2 != me_d)
         def _():
@@ -499,12 +514,6 @@
         @pl.when(late[t] * 4 + z // 2 != me_d)
         def _():
             wl_copy(t).wait_send()
-
-    def drain(i, carry):
-        a_copy((me_d + i) % DP).wait_send()
-        return carry
-
-    lax.fori_loop(1, DP, drain, 0)
 
 
 def hand_over(wg_in, tg_in, wg_out, tg_out):

time: 67.5 us -> 65.5 us (0.970)
  the two profiles are of different devices: /device:TPU:38 before, /device:TPU:55 now
where the time goes in v5:
time: 65.5 us; the launch traced here: 65.4 us
  Pallas kernels  64.7 us (99%)
    pallas_call x1, Pallas kernels, on_device(): pl.pallas_call(kernel, out_shape=(pltpu.VMEM((2 * PAIRS, 256), BF), pltpu...  64 us

profile of v5, /device:TPU:55, one launch (start us, length us, event | category | flops | bytes accessed | tf_op | source)
XLA Modules:
  0.0 65.4 jit_solution(4867244436966275887)
XLA Ops:
  0.6 64.0 %shard_map.86 = (bf16[240,256]{1,0:T(8,128)(2,1)S(1)}, f32[512,128]{1,0:T(8,128)S(1)}) custom-call(bf16[2,128,1024]{2,1,0:T(8,128)(2,1)} %emb_hbm.1, bf16[128,1024]{1,0:T(8,128)(2,1)} %cot_ref.1, bf16[240,8192]{1,0:T(8,128)(2,1)} %w_ref.1, s32[16,128]{1,0:T(8,128)} %bitcast.1, bf16[256,256]{1,0:T(8,128)(2,1)} %constant.6.clone.spread_hbm, ...), custom_call_target="tpu_custom_call" | custom-call | tf_op jit(solution)/shard_map/pallas_call | solution.py:530
  64.6 0.8 %shard_map.87 = (bf16[240,256]{1,0:T(8,128)(2,1)}, f32[512,128]{1,0:T(8,128)}) custom-call(bf16[240,256]{1,0:T(8,128)(2,1)S(1)} %get-tuple-element.4.wg_in, f32[512,128]{1,0:T(8,128)S(1)} %get-tuple-element.5.tg_in), custom_call_target="tpu_custom_call" | custom-call | tf_op jit(solution)/shard_map/pallas_call | solution.py:570

commit v6 on v5

--- a/solution.py
+++ b/solution.py
@@ -428,6 +428,12 @@
         tg_ref[...] += dot(jnp.concatenate(hots, axis=1), values)
         return carry
 
+    for i in range(1, 8):
+        block = x_v.at[core, yh, (z + 8 - i) % 8, pl.ds(0, XROWS)]
+        rcopy(block, block, x_ss.at[0], x_rs.at[(z + 8 - i) % 8], dp=twin).wait_recv()
+    x_half = x_v.at[core, yh, :, pl.ds(0, XROWS)]
+    start(rcopy(x_half, x_half, x_ss.at[8], x_rs.at[8], dp=y_part))
+
     ag_wait(1, 7, cz_v.at[left_o])
     ag(1, 9, cz_v.at[left_o, 0], right)
     ag_wait(1, 8, cz_v.at[right_o])
@@ -437,12 +443,6 @@
     ag_opp_o(1, cz_v)
     wl_make(0)
     settle()
-    for i in range(1, 8):
-        block = x_v.at[core, yh, (z + 8 - i) % 8, pl.ds(0, XROWS)]
-        rcopy(block, block, x_ss.at[0], x_rs.at[(z + 8 - i) % 8], dp=twin).wait_recv()
-    x_half = x_v.at[core, yh, :, pl.ds(0, XROWS)]
-    start(rcopy(x_half, x_half, x_ss.at[8], x_rs.at[8], dp=y_part))
-
     ws_make(opp)
     lax.fori_loop(0, 4, a_add, 0)
 

time: 65.5 us -> 62.4 us (0.953)
  the two profiles are of different devices: /device:TPU:55 before, /device:TPU:1 now
where the time goes in v6:
time: 62.4 us; the launch traced here: 62.1 us
  Pallas kernels  61.5 us (99%)
  between operations  0.64 us (1%)
    pallas_call x1, Pallas kernels, on_device(): pl.pallas_call(kernel, out_shape=(pltpu.VMEM((2 * PAIRS, 256), BF), pltpu...  60.7 us

profile of v6, /device:TPU:1, one launch (start us, length us, event | category | flops | bytes accessed | tf_op | source)
XLA Modules:
  0.0 62.1 jit_solution(6704530823044935304)
XLA Ops:
  0.6 60.7 %shard_map.86 = (bf16[240,256]{1,0:T(8,128)(2,1)S(1)}, f32[512,128]{1,0:T(8,128)S(1)}) custom-call(bf16[2,128,1024]{2,1,0:T(8,128)(2,1)} %emb_hbm.1, bf16[128,1024]{1,0:T(8,128)(2,1)} %cot_ref.1, bf16[240,8192]{1,0:T(8,128)(2,1)} %w_ref.1, s32[16,128]{1,0:T(8,128)} %bitcast.1, bf16[256,256]{1,0:T(8,128)(2,1)} %constant.6.clone.spread_hbm, ...), custom_call_target="tpu_custom_call" | custom-call | tf_op jit(solution)/shard_map/pallas_call | solution.py:530
  61.4 0.8 %shard_map.87 = (bf16[240,256]{1,0:T(8,128)(2,1)}, f32[512,128]{1,0:T(8,128)}) custom-call(bf16[240,256]{1,0:T(8,128)(2,1)S(1)} %get-tuple-element.4.wg_in, f32[512,128]{1,0:T(8,128)S(1)} %get-tuple-element.5.tg_in), custom_call_target="tpu_custom_call" | custom-call | tf_op jit(solution)/shard_map/pallas_call | solution.py:570

commit v7 on v6

--- a/solution.py
+++ b/solution.py
@@ -440,10 +440,10 @@
     ag(1, 10, cz_v.at[right_o, 1], left)
     wl_make(1)
     wl_make(2)
+    ws_make(opp)
     ag_opp_o(1, cz_v)
     wl_make(0)
     settle()
-    ws_make(opp)
     lax.fori_loop(0, 4, a_add, 0)
 
     other = x_v.at[core, 1 - yh, :, pl.ds(0, XROWS)]

time: 62.4 us -> 62.4 us (level)
  no operation moved by 1% of the time
where the time goes in v7:
time: 62.4 us; the launch traced here: 62.1 us
  Pallas kernels  61.5 us (99%)
  between operations  0.64 us (1%)
    pallas_call x1, Pallas kernels, on_device(): pl.pallas_call(kernel, out_shape=(pltpu.VMEM((2 * PAIRS, 256), BF), pltpu...  60.7 us

profile of v7, /device:TPU:1, one launch (start us, length us, event | category | flops | bytes accessed | tf_op | source)
XLA Modules:
  0.0 62.1 jit_solution(3982355820753738764)
XLA Ops:
  0.6 60.7 %shard_map.86 = (bf16[240,256]{1,0:T(8,128)(2,1)S(1)}, f32[512,128]{1,0:T(8,128)S(1)}) custom-call(bf16[2,128,1024]{2,1,0:T(8,128)(2,1)} %emb_hbm.1, bf16[128,1024]{1,0:T(8,128)(2,1)} %cot_ref.1, bf16[240,8192]{1,0:T(8,128)(2,1)} %w_ref.1, s32[16,128]{1,0:T(8,128)} %bitcast.1, bf16[256,256]{1,0:T(8,128)(2,1)} %constant.6.clone.spread_hbm, ...), custom_call_target="tpu_custom_call" | custom-call | tf_op jit(solution)/shard_map/pallas_call | solution.py:530
  61.3 0.8 %shard_map.87 = (bf16[240,256]{1,0:T(8,128)(2,1)}, f32[512,128]{1,0:T(8,128)}) custom-call(bf16[240,256]{1,0:T(8,128)(2,1)S(1)} %get-tuple-element.4.wg_in, f32[512,128]{1,0:T(8,128)S(1)} %get-tuple-element.5.tg_in), custom_call_target="tpu_custom_call" | custom-call | tf_op jit(solution)/shard_map/pallas_call | solution.py:570
